TPU v7x, 768 devices: a whole 4x8x12 slice. The times are simulated.
768 devices in a mesh: morton: 192 (over y, z, core), sub: 4 (over x).
Axes of the slice: x: 4, y: 8, z: 12, core: 2. Of those that a mesh axis runs over, the one named last changes fastest.
Arguments:
- direction: float32 [49152, 3, 512], P(('morton', 'sub')), may hold values from -6 to 6
- jacobian: float32 [49152, 512], P(('morton', 'sub')), may hold values from 0.8 to 1.25
- shear_modulus: float32 [49152], P(('morton', 'sub')), may hold values from 0.5 to 2
- lame_modulus: float32 [49152], P(('morton', 'sub')), may hold values from 0.4 to 1.6
- refine_level: int32 [49152], P(('morton', 'sub')), may hold values from 1 to 2, as said below
- live_flag: int32 [49152], P(('morton', 'sub')), may hold values from 0 to 1, as said below
- neighbor: int32 [49152, 6], P(('morton', 'sub')), may hold values from 0 to 49151, as said below
- face_kind: int32 [49152, 6], P(('morton', 'sub')), may hold values from 0 to 2, as said below
- face_quadrant: int32 [49152, 6], P(('morton', 'sub')), may hold values from 0 to 3
Outputs:
- hessian_product: float32 [49152, 3, 512], P(('morton', 'sub'))
Inputs may be any that keep to these rules, and one draw needn't show every extreme that they name: `neighbor`: each entry names a live block whose device's index along morton differs from the block's own by at most one. The 384 entries of one device's blocks name blocks of any single device at most 64 times; the devices of the first Morton range reach that. `live_flag`: A device's live blocks come first among its 64 blocks; each device has at least a quarter of its blocks live, and some devices, the last one among them, have all live. The grid spacing of a block is 2 ** (-refine_level) relative to level 0. `face_kind`: 2 exactly where the neighbour's refine_level is one less than the block's own, 1 where the two are equal, 0 where the neighbour is finer.
All inputs are finite; a program needn't handle non-finite values.
Results may differ from a plain program's by a relative error of at most 0.00005.
Values sent between devices are 32-bit elements; how exact they have to be, the bound alone decides.
A program may use at most 32 MiB of HBM per device.

v0:
```python
import jax
import jax.numpy as jnp
from jax import lax
from jax.sharding import PartitionSpec as P


def extended_2(block, sides, width):
    for axis, dim in sides:
        count = lax.axis_size(axis)
        forward = [(i, i + 1) for i in range(count - 1)]
        backward = [(target, source) for source, target in forward]
        low = lax.ppermute(
            lax.slice_in_dim(block, block.shape[dim] - width, None, axis=dim), axis, forward
        )
        high = lax.ppermute(lax.slice_in_dim(block, 0, width, axis=dim), axis, backward)
        block = jnp.concatenate([low, block, high], axis=dim)
    return block


def face_layers(nodal):
    blocks = nodal.shape[0]
    cube = nodal.reshape(blocks, 3, 8, 8, 8)
    layer_list = [
        cube[:, :, 0],
        cube[:, :, 7],
        cube[:, :, :, 0],
        cube[:, :, :, 7],
        cube[:, :, :, :, 0],
        cube[:, :, :, :, 7],
    ]
    return jnp.stack([layer.reshape(blocks, 3, 64) for layer in layer_list], axis=1)


def prolong_tables():
    fine = jnp.arange(8, dtype=jnp.int32)
    coarse = jnp.arange(8, dtype=jnp.int32)
    halves = []
    for upper_part in range(2):
        doubled = 7 * upper_part + fine
        lower_hit = ((doubled // 2)[:, None] == coarse[None, :]).astype(jnp.float32)
        upper_hit = (((doubled + 1) // 2)[:, None] == coarse[None, :]).astype(jnp.float32)
        halves.append(0.5 * lower_hit + 0.5 * upper_hit)
    return jnp.stack([jnp.kron(halves[quad // 2], halves[quad % 2]) for quad in range(4)])


def quadrant_pick(spread, face_quadrant):
    picks = (
        jnp.arange(4, dtype=jnp.int32)[:, None, None, None, None]
        == face_quadrant[None, :, :, None, None]
    )
    return jnp.sum(jnp.where(picks, spread, jnp.zeros_like(spread)), axis=0)


def fill_ghost(raw_ghost, face_kind, face_quadrant):
    spread = jnp.einsum(
        "xpq,bfcq->xbfcp", prolong_tables(), raw_ghost, precision=lax.Precision.HIGHEST
    )
    hanging = quadrant_pick(spread, face_quadrant)
    kind_mask = face_kind[:, :, None, None]
    return jnp.where(
        kind_mask == 1, raw_ghost, jnp.where(kind_mask == 2, hanging, jnp.zeros_like(raw_ghost))
    )


def unfill_ghost(ghost_bar, face_kind, face_quadrant):
    spread = jnp.einsum(
        "xpq,bfcp->xbfcq", prolong_tables(), ghost_bar, precision=lax.Precision.HIGHEST
    )
    hanging = quadrant_pick(spread, face_quadrant)
    kind_mask = face_kind[:, :, None, None]
    return jnp.where(
        kind_mask == 1, ghost_bar, jnp.where(kind_mask == 2, hanging, jnp.zeros_like(ghost_bar))
    )


def gradient(nodal, ghost_vals, block_scale):
    blocks = nodal.shape[0]
    cube = nodal.reshape(blocks, 3, 8, 8, 8)
    pieces = []
    for axis_id in range(3):
        low_side = jnp.expand_dims(ghost_vals[:, 2 * axis_id].reshape(blocks, 3, 8, 8), 2 + axis_id)
        high_side = jnp.expand_dims(
            ghost_vals[:, 2 * axis_id + 1].reshape(blocks, 3, 8, 8), 2 + axis_id
        )
        padded = jnp.concatenate([low_side, cube, high_side], axis=2 + axis_id)
        ahead = lax.slice_in_dim(padded, 2, 10, axis=2 + axis_id)
        behind = lax.slice_in_dim(padded, 0, 8, axis=2 + axis_id)
        pieces.append((0.5 * (ahead - behind)).reshape(blocks, 3, 512))
    strain = jnp.stack(pieces, axis=2)
    return strain * block_scale[:, None, None, None]


def stress_of(strain, jacobian, shear_modulus, lame_modulus):
    volume_change = strain[:, 0, 0] + strain[:, 1, 1] + strain[:, 2, 2]
    shear_mod = shear_modulus[:, None] - lame_modulus[:, None] * jnp.log(jacobian)
    symmetric = strain + jnp.swapaxes(strain, 1, 2)
    identity = jnp.eye(3, dtype=jnp.float32)
    return (
        lame_modulus[:, None, None, None]
        * volume_change[:, None, None, :]
        * identity[None, :, :, None]
        + shear_mod[:, None, None, :] * symmetric
    )


def per_device(
    direction,
    jacobian,
    shear_modulus,
    lame_modulus,
    refine_level,
    live_flag,
    neighbor,
    face_kind,
    face_quadrant,
):
    blocks = direction.shape[0]
    groups = lax.axis_size("sub")
    position = lax.axis_index("morton")
    block_scale = 0.5 * jnp.exp2(refine_level.astype(jnp.float32))
    live_mask = live_flag.astype(jnp.float32)
    masked = direction * live_mask[:, None, None]
    own_faces = face_layers(masked).reshape(blocks, 1152)
    opposite = jnp.array([1, 0, 3, 2, 5, 4], dtype=jnp.int32)
    target_dev = neighbor // blocks
    range_faces = lax.all_gather(own_faces, "sub", axis=0, tiled=True)
    ghost_table = extended_2(range_faces[None], (("morton", 0),), 1)
    slot_row = (
        (target_dev // groups - position + 1) * groups + target_dev % groups
    ) * blocks + neighbor % blocks
    slot_index = (slot_row * 6 + opposite[None, :]).reshape(-1)
    flat_table = ghost_table.reshape(3 * groups * blocks * 6, 192)
    raw_ghost = jnp.take(flat_table, slot_index, axis=0).reshape(blocks, 6, 3, 64)
    ghost_vals = fill_ghost(raw_ghost, face_kind, face_quadrant)

    def local_strain(nodal, ghost_part):
        return gradient(nodal, ghost_part, block_scale)

    strain, pullback = jax.vjp(local_strain, masked, ghost_vals)
    stress = stress_of(strain, jacobian, shear_modulus, lame_modulus)
    nodal_bar, ghost_bar = pullback(stress)
    outgoing = unfill_ghost(ghost_bar, face_kind, face_quadrant).reshape(blocks * 6, 192)
    contrib = jnp.zeros((3 * groups * blocks * 6, 192), jnp.float32).at[slot_index].add(outgoing)
    contrib = contrib.reshape(3, groups * blocks, 1152)
    extended = extended_2(contrib, (("morton", 0),), 1)
    incoming = extended[0] + extended[2] + extended[4]
    returned = lax.psum_scatter(incoming, "sub", scatter_dimension=0, tiled=True)
    _, spread_back = jax.vjp(face_layers, masked)
    (landed,) = spread_back(returned.reshape(blocks, 6, 3, 64))
    return (nodal_bar + landed) * live_mask[:, None, None]


def solution(mesh):
    in_specs = (
        P(("morton", "sub"), None, None),
        P(("morton", "sub"), None),
        P(("morton", "sub")),
        P(("morton", "sub")),
        P(("morton", "sub")),
        P(("morton", "sub")),
        P(("morton", "sub"), None),
        P(("morton", "sub"), None),
        P(("morton", "sub"), None),
    )
    out_specs = P(("morton", "sub"), None, None)
    return jax.shard_map(
        per_device, mesh=mesh, in_specs=in_specs, out_specs=out_specs, check_vma=False
    )
```

profile of v0, /device:TPU:8, one launch (start us, length us, event | category | flops | bytes accessed | tf_op | source)
XLA Modules:
  0.0 189.7 jit_solution(4149577426751592158)
XLA Ops:
  6.5 0.7 convert_element_type.10
  7.2 1.3 copy.66
  8.8 0.7 copy-done.2
  9.6 0.9 copy.107
  10.6 0.6 compare_and_fusion
  11.6 0.8 copy.82
  12.6 37.2 %all-gather.2.cloned.1.call-done = f32[256,1152]{1,0:T(8,128)} async-done(((f32[64,1152]{1,0:T(8,128)}), f32[256,1152]{1,0:T(8,128)}) %all-gather.2.cloned.1.call-update) | async-done | bytes 1179664 | tf_op jit(solution)/shard_map/all_gather | solution.py:126
  49.8 5.0 %collective-permute-start.1 = (f32[1,256,1152]{2,1,0:T(8,128)}, f32[1,256,1152]{2,1,0:T(8,128)S(1)}, u32[]{:S(2)}, u32[]{:S(2)}) collective-permute-start(f32[1,256,1152]{2,1,0:T(8,128)} %bitcast.141), channel_id=1, source_target_pairs={{4,0},{8,4},{12,8},{16,12},{20,16},{24,20},{28,24},{32,28},{36,32}... | collective-permute-start | bytes 3538952 | tf_op jit(solution)/shard_map/ppermute | solution.py:15
  54.8 1.9 %collective-permute-start = (f32[1,256,1152]{2,1,0:T(8,128)}, f32[1,256,1152]{2,1,0:T(8,128)}, u32[]{:S(2)}, u32[]{:S(2)}) collective-permute-start(f32[1,256,1152]{2,1,0:T(8,128)} %bitcast.142), channel_id=1, source_target_pairs={{0,4},{4,8},{8,12},{12,16},{16,20},{20,24},{24,28},{28,32},{32,36}... | collective-permute-start | bytes 3538952 | tf_op jit(solution)/shard_map/ppermute | solution.py:12
  57.0 0.7 mul.289
  57.7 0.7 mul.292
  58.5 0.7 mul.284
  59.2 0.8 mul.294
  61.1 7.7 %collective-permute-done.1 = f32[1,256,1152]{2,1,0:T(8,128)S(1)} collective-permute-done((f32[1,256,1152]{2,1,0:T(8,128)}, f32[1,256,1152]{2,1,0:T(8,128)S(1)}, u32[]{:S(2)}, u32[]{:S(2)}) %collective-permute-start.1) | collective-permute-done | bytes 1179680 | tf_op jit(solution)/shard_map/ppermute | solution.py:15
  68.9 1.0 copy-done.4
  69.9 4.9 %collective-permute-done = f32[1,256,1152]{2,1,0:T(8,128)} collective-permute-done((f32[1,256,1152]{2,1,0:T(8,128)}, f32[1,256,1152]{2,1,0:T(8,128)}, u32[]{:S(2)}, u32[]{:S(2)}) %collective-permute-start) | collective-permute-done | bytes 1179680 | tf_op jit(solution)/shard_map/ppermute | solution.py:12
  74.8 2.2 %pad_maximum_fusion = f32[3,256,1152]{2,1,0:T(8,128)S(1)} fusion(f32[1,256,1152]{2,1,0:T(8,128)} %copy-done.4, f32[1,256,1152]{2,1,0:T(8,128)} %bitcast.143, f32[1,256,1152]{2,1,0:T(8,128)} %collective-permute-done), kind=kLoop, calls=%fused_computation.2 | loop fusion | flops 1769472 | bytes 7077888 | tf_op jit(solution)/shard_map/concatenate | solution.py:16
  77.0 3.5 %reshape.484 = f32[4608,192]{1,0:T(8,128)} reshape(f32[3,256,1152]{2,1,0:T(8,128)S(1)} %pad_maximum_fusion) | data formatting | bytes 7077888 | tf_op jit(solution)/shard_map/reshape | solution.py:132
  80.5 4.0 %gather_fusion = f32[384,192]{1,0:T(8,128)S(1)} fusion(f32[4608,192]{1,0:T(8,128)} %reshape.484, s32[1024]{0:T(1024)S(1)} %pad_clamp_fusion), kind=kCustom, calls=%fused_computation | custom fusion | bytes 591360 | tf_op jit(solution)/shard_map/jit(_take)/gather | solution.py:133
  84.9 2.4 %fusion.4 = f32[64,6,3,64]{3,0,2,1:T(8,128)S(1)} fusion(pred[4,64,6]{1,0,2:T(4,128)(4,1)S(1)} %copy-done.20, f32[64,6,3,64]{3,2,1,0:T(4,128)S(1)} %gather.7, pred[64,6]{0,1:T(8,128)(4,1)S(1)} %copy-done.16, f32[1,64,64]{2,1,0:T(8,128)S(1)} %copy-done.14, f32[1,64,64]{2,1,0:T(8,128)S(1)} %copy-done.12, f32[1,64,64]{2,1,0:T(8,128)S(1)} %copy-done.11, ...), kind=kOutput, calls=%fused_computation.11 | convolution fusion | flops 227131392 | bytes 657280 | tf_op jit(solution)/shard_map/xpq,bfcq->xbfcp/dot_general | solution.py:55
  90.9 0.9 copy-done
  92.0 0.7 copy.84
  92.7 0.7 copy.85
  93.6 0.9 copy-done.1
  94.5 0.7 copy.86
  95.2 0.7 copy.87
  96.0 3.3 %fusion = f32[64,6,3,64]{3,0,2,1:T(8,128)S(1)} fusion(pred[4,64,6]{1,0,2:T(4,128)(4,1)S(1)} %copy-done.21, f32[64,1,3,64]{3,0,2,1:T(8,128)S(1)} %copy.89, f32[64,1,3,64]{3,0,2,1:T(8,128)S(1)} %copy.88, f32[64,1,3,64]{3,0,2,1:T(8,128)} %copy.87, f32[64,1,3,64]{3,0,2,1:T(8,128)} %copy.86, f32[64,1,3,64]{3,0,2,1:T(8,128)} %copy.85, f32[64,1,3,64]{3,0,2,1:T(8,128)} %copy.84, ...), kind=kOutput, calls=%fused_computation.5 | convolution fusion | flops 227426304 | bytes 656896 | tf_op jit(solution)/shard_map/xpq,bfcp->xbfcq/dot_general | solution.py:66
  99.5 1.3 copy.90
  100.8 1.6 reshape.509
  102.3 5.2 %scatter_custom_fusion = f32[4608,192]{1,0:T(8,128)} fusion(s32[384]{0:T(512)} %copy-done.15, f32[384,192]{1,0:T(8,128)S(1)} %reshape.509, f32[]{:T(128)} %constant.136.clone.1), kind=kCustom, calls=%fused_computation.12 | custom fusion | flops 73728 | bytes 3539456 | tf_op jit(solution)/shard_map/scatter-add | solution.py:143
  107.5 4.6 %fusion.57 = (f32[1536,192]{1,0:T(8,128)}, f32[1536,192]{1,0:T(8,128)}, f32[1536,192]{1,0:T(8,128)}) fusion(f32[4608,192]{1,0:T(8,128)} %scatter_custom_fusion), kind=kLoop, calls=%fused_computation.152 | loop fusion | bytes 7077888 | tf_op jit(solution)/shard_map/slice | solution.py:13
  112.1 2.8 %slice.107 = f32[1,256,1152]{2,1,0:T(8,128)} reshape(f32[1536,192]{1,0:T(8,128)} %get-tuple-element.7) | data formatting | bytes 2359296 | tf_op jit(solution)/shard_map/slice | solution.py:13
  114.9 2.7 %slice.110 = f32[1,256,1152]{2,1,0:T(8,128)} reshape(f32[1536,192]{1,0:T(8,128)} %get-tuple-element.8) | data formatting | bytes 2359296 | tf_op jit(solution)/shard_map/slice | solution.py:15
  117.6 1.9 %collective-permute-start.3 = (f32[1,256,1152]{2,1,0:T(8,128)}, f32[1,256,1152]{2,1,0:T(8,128)}, u32[]{:S(2)}, u32[]{:S(2)}) collective-permute-start(f32[1,256,1152]{2,1,0:T(8,128)} %slice.110), channel_id=1, source_target_pairs={{4,0},{8,4},{12,8},{16,12},{20,16},{24,20},{28,24},{32,28},{36,32}... | collective-permute-start | bytes 3538952 | tf_op jit(solution)/shard_map/ppermute | solution.py:15
  119.5 2.4 %collective-permute-start.2 = (f32[1,256,1152]{2,1,0:T(8,128)}, f32[1,256,1152]{2,1,0:T(8,128)}, u32[]{:S(2)}, u32[]{:S(2)}) collective-permute-start(f32[1,256,1152]{2,1,0:T(8,128)} %slice.107), channel_id=1, source_target_pairs={{0,4},{4,8},{8,12},{12,16},{16,20},{20,24},{24,28},{28,32},{32,36}... | collective-permute-start | bytes 3538952 | tf_op jit(solution)/shard_map/ppermute | solution.py:12
  121.9 2.7 %squeeze.37 = f32[256,1152]{1,0:T(8,128)} reshape(f32[1536,192]{1,0:T(8,128)} %get-tuple-element.9) | data formatting | bytes 2359296 | tf_op jit(solution)/shard_map/squeeze | solution.py:146
  124.7 8.9 %collective-permute-done.3 = f32[1,256,1152]{2,1,0:T(8,128)} collective-permute-done((f32[1,256,1152]{2,1,0:T(8,128)}, f32[1,256,1152]{2,1,0:T(8,128)}, u32[]{:S(2)}, u32[]{:S(2)}) %collective-permute-start.3) | collective-permute-done | bytes 1179680 | tf_op jit(solution)/shard_map/ppermute | solution.py:15
  133.5 5.9 %collective-permute-done.2 = f32[1,256,1152]{2,1,0:T(8,128)} collective-permute-done((f32[1,256,1152]{2,1,0:T(8,128)}, f32[1,256,1152]{2,1,0:T(8,128)}, u32[]{:S(2)}, u32[]{:S(2)}) %collective-permute-start.2) | collective-permute-done | bytes 1179680 | tf_op jit(solution)/shard_map/ppermute | solution.py:12
  139.5 3.2 %bitcast_add_fusion.1 = f32[256,1152]{1,0:T(8,128)} fusion(f32[1,256,1152]{2,1,0:T(8,128)} %collective-permute-done.3, f32[256,1152]{1,0:T(8,128)} %squeeze.37, f32[1,256,1152]{2,1,0:T(8,128)} %collective-permute-done.2), kind=kLoop, calls=%fused_computation.18 | loop fusion | flops 589824 | bytes 4718592 | tf_op jit(solution)/shard_map/add | solution.py:146
  142.7 27.0 %reduce-scatter.2.cloned.1.call-done = f32[64,1152]{1,0:T(8,128)} async-done(((f32[256,1152]{1,0:T(8,128)}), f32[64,1152]{1,0:T(8,128)}) %reduce-scatter.2.cloned.1.call-update) | async-done | bytes 294928 | tf_op jit(solution)/shard_map/reduce_scatter | solution.py:147
  169.6 2.2 %reshape.496 = f32[64,6,3,64]{3,2,1,0:T(4,128)} reshape(f32[64,1152]{1,0:T(8,128)} %reduce-scatter.2.cloned.1.call-done) | data formatting | bytes 589824 | tf_op jit(solution)/shard_map/reshape | solution.py:149
  171.8 2.1 %fusion.58 = (f32[64,1,3,64]{3,2,1,0:T(4,128)}, f32[64,1,3,64]{3,2,1,0:T(4,128)}, f32[64,1,3,64]{3,2,1,0:T(4,128)}, f32[64,1,3,64]{3,2,1,0:T(4,128)S(1)}, f32[64...) fusion(f32[64,6,3,64]{3,2,1,0:T(4,128)} %reshape.496), kind=kLoop, calls=%fused_computation.153 | loop fusion | bytes 589824 | tf_op jit(solution)/shard_map/transpose(jvp())/unstack | solution.py:31
  173.9 1.6 copy.91
  175.5 1.6 copy.101
  177.2 1.6 copy.99
  178.8 0.8 copy.97
  179.8 2.0 %fusion.10 = f32[64,3,8,8,8]{0,4,3,2,1:T(8,128)S(1)} fusion(f32[64,3,8,8,8]{0,4,3,2,1:T(8,128)} %copy-done.1, f32[64,3,8,8,8]{0,4,3,2,1:T(8,128)S(1)} %bitcast.131, f32[64,3,8,8,8]{0,4,3,2,1:T(8,128)S(1)} %neg.11, f32[64,3,8,8,8]{0,4,3,2,1:T(8,128)S(1)} %bitcast.128, f32[64,3,8,8,8]{0,4,3,2,1:T(8,128)} %copy-done, f32[64,3,8,8,8]{0,4,3,2,1:T(8,128)S(1)} %bitcast.125, ...), kind=kLoop, calls=%fused_computation.31 | loop fusion | flops 1081344 | bytes 3047424 | tf_op jit(solution)/shard_map/add | solution.py:150
  181.9 1.0 copy.103
  (107 shorter events, 6.6 us)
Async XLA Ops:
  6.5 43.3 %all-gather.2.cloned.1.call-start = ((), (), s32[]{:S(2)}) async-start(), calls=%async_computation.1 | async-start | bytes 1474560 | tf_op jit(solution)/shard_map/all_gather | solution.py:126
  7.2 3.3 %copy-start.24 = (f32[64]{0:T(128)}, f32[64]{0:T(128)S(1)}, u32[]{:S(2)}) copy-start(f32[64]{0:T(128)S(1)} %convert_element_type.10) | copy-start | bytes 772
  8.5 2.1 %copy-start.18 = (s32[64,6]{0,1:T(8,128)S(1)}, s32[64,6]{0,1:T(8,128)}, u32[]{:S(2)}) copy-start(s32[64,6]{0,1:T(8,128)} %param.16) | copy-start | bytes 4612
  8.5 2.1 %copy-start.19 = (s32[64,6]{0,1:T(8,128)S(1)}, s32[64,6]{0,1:T(8,128)}, u32[]{:S(2)}) copy-start(s32[64,6]{0,1:T(8,128)} %param.17) | copy-start | bytes 4612
  8.5 2.1 %copy-start.28 = (s32[6]{0:T(128)S(1)}, s32[6]{0:T(128)}, u32[]{:S(2)}) copy-start(s32[6]{0:T(128)} %constant.140.clone) | copy-start | bytes 76
  8.5 3.0 %copy-start.10 = (f32[64,512]{1,0:T(8,128)S(1)}, f32[64,512]{1,0:T(8,128)}, u32[]{:S(2)}) copy-start(f32[64,512]{1,0:T(8,128)} %param.11) | copy-start | bytes 393220
  8.5 3.0 %copy-start.22 = (f32[64]{0:T(128)S(1)}, f32[64]{0:T(128)}, u32[]{:S(2)}) copy-start(f32[64]{0:T(128)} %param.13) | copy-start | bytes 772
  8.5 3.0 %copy-start.27 = (f32[64]{0:T(128)S(1)}, f32[64]{0:T(128)}, u32[]{:S(2)}) copy-start(f32[64]{0:T(128)} %param.12) | copy-start | bytes 772
  8.6 0.9 copy-start.2
  9.5 50.5 %copy-start.29 = (s32[64]{0:T(128)S(1)}, s32[64]{0:T(128)}, u32[]{:S(2)}) copy-start(s32[64]{0:T(128)} %param.14) | copy-start | bytes 772
  9.5 51.0 %copy-start.17 = (s32[64,6]{0,1:T(8,128)S(1)}, s32[64,6]{0,1:T(8,128)}, u32[]{:S(2)}) copy-start(s32[64,6]{0,1:T(8,128)} %param.18) | copy-start | bytes 4612
  10.5 159.1 %reduce-scatter.2.cloned.1.call-start = ((), (), s32[]{:S(2)}) async-start(), calls=%async_computation.2 | async-start | bytes 1474560 | tf_op jit(solution)/shard_map/reduce_scatter | solution.py:147
  49.8 19.1 %collective-permute-start.1 = (f32[1,256,1152]{2,1,0:T(8,128)}, f32[1,256,1152]{2,1,0:T(8,128)S(1)}, u32[]{:S(2)}, u32[]{:S(2)}) collective-permute-start(f32[1,256,1152]{2,1,0:T(8,128)} %bitcast.141), channel_id=1, source_target_pairs={{4,0},{8,4},{12,8},{16,12},{20,16},{24,20},{28,24},{32,28},{36,32}... | collective-permute-start | bytes 3538952 | tf_op jit(solution)/shard_map/ppermute | solution.py:15
  54.8 19.9 %collective-permute-start = (f32[1,256,1152]{2,1,0:T(8,128)}, f32[1,256,1152]{2,1,0:T(8,128)}, u32[]{:S(2)}, u32[]{:S(2)}) collective-permute-start(f32[1,256,1152]{2,1,0:T(8,128)} %bitcast.142), channel_id=1, source_target_pairs={{0,4},{4,8},{8,12},{12,16},{16,20},{20,24},{24,28},{28,32},{32,36}... | collective-permute-start | bytes 3538952 | tf_op jit(solution)/shard_map/ppermute | solution.py:12
  60.0 8.9 %copy-start.15 = (s32[384]{0:T(512)}, s32[384]{0:T(512)S(1)}, u32[]{:S(2)}) copy-start(s32[384]{0:T(512)S(1)} %fusion.51) | copy-start | bytes 4612
  68.9 1.0 copy-start.4
  80.5 4.3 %copy-start.11 = (f32[1,64,64]{2,1,0:T(8,128)S(1)}, f32[1,64,64]{2,1,0:T(8,128)}, u32[]{:S(2)}) copy-start(f32[1,64,64]{2,1,0:T(8,128)} %mul.289) | copy-start | bytes 49156
  80.5 4.3 %copy-start.12 = (f32[1,64,64]{2,1,0:T(8,128)S(1)}, f32[1,64,64]{2,1,0:T(8,128)}, u32[]{:S(2)}) copy-start(f32[1,64,64]{2,1,0:T(8,128)} %mul.292) | copy-start | bytes 49156
  80.5 4.3 %copy-start.13 = (f32[1,64,64]{2,1,0:T(8,128)S(1)}, f32[1,64,64]{2,1,0:T(8,128)}, u32[]{:S(2)}) copy-start(f32[1,64,64]{2,1,0:T(8,128)} %mul.284) | copy-start | bytes 49156
  80.5 4.4 %copy-start.14 = (f32[1,64,64]{2,1,0:T(8,128)S(1)}, f32[1,64,64]{2,1,0:T(8,128)}, u32[]{:S(2)}) copy-start(f32[1,64,64]{2,1,0:T(8,128)} %mul.294) | copy-start | bytes 49156
  80.5 4.4 %copy-start.16 = (pred[64,6]{0,1:T(8,128)(4,1)S(1)}, pred[64,6]{0,1:T(8,128)(4,1)}, u32[]{:S(2)}) copy-start(pred[64,6]{0,1:T(8,128)(4,1)} %get-tuple-element.5) | copy-start | bytes 1156
  80.5 4.4 %copy-start.20 = (pred[4,64,6]{1,0,2:T(4,128)(4,1)S(1)}, pred[4,64,6]{1,0,2:T(4,128)(4,1)}, u32[]{:S(2)}) copy-start(pred[4,64,6]{1,0,2:T(4,128)(4,1)} %iota_compare_fusion) | copy-start | bytes 4612
  87.3 1.1 copy-start.3
  87.7 1.3 copy-start.26
  89.0 0.7 copy-start.23
  89.0 1.0 copy-start.5
  90.9 0.9 copy-start
  92.0 4.0 %copy-start.21 = (pred[4,64,6]{1,0,2:T(4,128)(4,1)S(1)}, pred[4,64,6]{1,0,2:T(4,128)(4,1)}, u32[]{:S(2)}) copy-start(pred[4,64,6]{1,0,2:T(4,128)(4,1)} %iota_compare_fusion) | copy-start | bytes 4612
  93.5 0.9 copy-start.1
  95.2 4.0 %copy-start.6 = (f32[64,1,3,64]{3,0,2,1:T(8,128)S(1)}, f32[64,1,3,64]{3,0,2,1:T(8,128)}, u32[]{:S(2)}) copy-start(f32[64,1,3,64]{3,0,2,1:T(8,128)} %copy.84) | copy-start | bytes 147460
  96.0 3.3 %copy-start.7 = (f32[64,1,3,64]{3,0,2,1:T(8,128)S(1)}, f32[64,1,3,64]{3,0,2,1:T(8,128)}, u32[]{:S(2)}) copy-start(f32[64,1,3,64]{3,0,2,1:T(8,128)} %copy.85) | copy-start | bytes 147460
  96.0 3.3 %copy-start.8 = (f32[64,1,3,64]{3,0,2,1:T(8,128)S(1)}, f32[64,1,3,64]{3,0,2,1:T(8,128)}, u32[]{:S(2)}) copy-start(f32[64,1,3,64]{3,0,2,1:T(8,128)} %copy.86) | copy-start | bytes 147460
  96.0 3.3 %copy-start.9 = (f32[64,1,3,64]{3,0,2,1:T(8,128)S(1)}, f32[64,1,3,64]{3,0,2,1:T(8,128)}, u32[]{:S(2)}) copy-start(f32[64,1,3,64]{3,0,2,1:T(8,128)} %copy.87) | copy-start | bytes 147460
  117.6 15.9 %collective-permute-start.3 = (f32[1,256,1152]{2,1,0:T(8,128)}, f32[1,256,1152]{2,1,0:T(8,128)}, u32[]{:S(2)}, u32[]{:S(2)}) collective-permute-start(f32[1,256,1152]{2,1,0:T(8,128)} %slice.110), channel_id=1, source_target_pairs={{4,0},{8,4},{12,8},{16,12},{20,16},{24,20},{28,24},{32,28},{36,32}... | collective-permute-start | bytes 3538952 | tf_op jit(solution)/shard_map/ppermute | solution.py:15
  119.5 19.9 %collective-permute-start.2 = (f32[1,256,1152]{2,1,0:T(8,128)}, f32[1,256,1152]{2,1,0:T(8,128)}, u32[]{:S(2)}, u32[]{:S(2)}) collective-permute-start(f32[1,256,1152]{2,1,0:T(8,128)} %slice.107), channel_id=1, source_target_pairs={{0,4},{4,8},{8,12},{12,16},{16,20},{20,24},{24,28},{28,32},{32,36}... | collective-permute-start | bytes 3538952 | tf_op jit(solution)/shard_map/ppermute | solution.py:12
  179.8 2.0 %copy-start.25 = (f32[64]{0:T(128)S(1)}, f32[64]{0:T(128)}, u32[]{:S(2)}) copy-start(f32[64]{0:T(128)} %copy-done.24) | copy-start | bytes 772
Sparse Core Ops, SparseCore 0:
  10.7 39.0 all-gather.1
  142.8 26.7 reduce-scatter.1
where the time goes:
time: 190 us
  waiting for transfers between devices  91.7 us (48%)
  local copies, waits for them, and re-layouts  49.4 us (26%)
  other arithmetic  17.7 us (9%)
  between operations  14 us (7%)
  starting transfers between devices  11.3 us (6%)
  matrix products  5.65 us (3%)
    all_gather x1, waiting for transfers between devices, per_device(): range_faces = lax.all_gather(own_faces, 'sub', axis=0, tiled=True)  37.2 us
    reduce_scatter x1, waiting for transfers between devices, per_device(): lax.psum_scatter(incoming, 'sub', scatter_dimension=0, tiled=True)  27 us
    ppermute x2, waiting for transfers between devices, extended_2(): lax.ppermute(lax.slice_in_dim(block, 0, width, axis=dim), axis, backward)  16.6 us
    ppermute x2, waiting for transfers between devices, extended_2(): lax.ppermute(lax.slice_in_dim(block, block.shape[dim] - width, None, axis...  10.8 us
    another operation x8, local copies, waits for them, and re-layouts, face_layers(): jnp.stack([layer.reshape(blocks, 3, 64) for layer in layer_list], axis=1)  7.93 us
    slice x2, local copies, waits for them, and re-layouts, extended_2(): lax.slice_in_dim(block, block.shape[dim] - width, None, axis=dim)  7.39 us
    ppermute x2, starting transfers between devices, extended_2(): lax.ppermute(lax.slice_in_dim(block, 0, width, axis=dim), axis, backward)  6.95 us
    unnamed x66, local copies, waits for them, and re-layouts  5.9 us
  transfers between devices with their start and end apart: 6, of which 6 were waited for; matrix products, arithmetic and copies ran while one was open for 5% of the time, Pallas kernels for 0%

commit v1 on v0

v1 whole, which is shorter than its diff:
```python
import functools

import jax
import jax.numpy as jnp
import numpy as np
from jax import lax
from jax.experimental import pallas as pl
from jax.experimental.pallas import tpu as pltpu
from jax.sharding import PartitionSpec as P

BLOCKS = 64
ROWS = 6 * BLOCKS
PEERS = 12
SLOTS = PEERS * BLOCKS
SELF = 4
F32 = jnp.float32
BF16 = jnp.bfloat16
MESH = pl.DeviceIdType.MESH
GROUPS = ((2, 6, 10), (1, 3, 5, 7, 9, 11), (0, 8, 4))
ORDER = tuple(p for group in GROUPS for p in group)


def tables():
    node = np.arange(512)
    coords = (node // 64, (node // 8) % 8, node % 8)
    pick = np.zeros((512, 6, 64), np.float32)
    for face in range(6):
        axis = face // 2
        others = [coords[a] for a in range(3) if a != axis]
        for n in np.nonzero(coords[axis] == 7 * (face % 2))[0]:
            pick[n, face, others[0][n] * 8 + others[1][n]] = 1
    halves = np.zeros((2, 8, 8), np.float32)
    for u in range(2):
        for i in range(8):
            halves[u, i, (7 * u + i) // 2] += 0.5
            halves[u, i, (7 * u + i + 1) // 2] += 0.5
    fill = np.zeros((128, 512), np.float32)
    unfill = np.zeros((128, 512), np.float32)
    for q in range(4):
        spread = np.kron(halves[q // 2], halves[q % 2])
        for half in range(2):
            lanes = slice(64 * half, 64 * half + 64)
            cols = slice(128 * q + 64 * half, 128 * q + 64 * half + 64)
            fill[lanes, cols] = spread.T
            unfill[lanes, cols] = spread
    twice = np.concatenate([pick, pick], axis=2).reshape(512, 768)
    inject = pick.reshape(512, ROWS).T
    before = np.triu(np.ones((ROWS, ROWS), np.float32), 1)
    return [jnp.asarray(t, BF16) for t in (twice, inject, fill, unfill, before)]


def split(values):
    high = values.astype(BF16)
    low = (values - high.astype(F32)).astype(BF16)
    return high, low


def dot(a, b):
    return jnp.dot(a, b, preferred_element_type=F32)


def lane_iota(shape):
    return lax.broadcasted_iota(jnp.int32, shape, len(shape) - 1)


def kernel(
    ranges,
    x_hbm, jac_hbm, mu_hbm, lam_hbm, level_hbm, live_hbm, nb_hbm, kind_hbm, quad_hbm,
    twice_hbm, inject_hbm, fill_hbm, unfill_hbm, before_hbm,
    out_ref,
    x, jac, mu, lam, level, live, nb, kind, quad,
    twice, inject, fill, unfill, before,
    tile_s, code_b, coef, table, sel, sel_t, place, place_t, lists, lists_in,
    fsend, frecv, asend, arecv, landed_rows, sym, inj, back,
    in_sem, list_ssem, list_rsem, f_ssem, f_rsem, a_ssem, a_rsem,
):
    me_m = lax.axis_index("morton")
    me_x = lax.axis_index("sub")

    def device(p):
        dm, dx = p // 4 - 1, p % 4
        return (lax.rem(me_m + (dm + ranges), ranges), lax.rem(me_x + dx, 4))

    def mirror(p):
        return (2 - p // 4) * 4 + (4 - p % 4) % 4

    def remote(p, src, dst, ssem, rsem):
        return pltpu.make_async_remote_copy(
            src_ref=src, dst_ref=dst.at[mirror(p)], send_sem=ssem.at[p], recv_sem=rsem.at[mirror(p)],
            device_id=device(p), device_id_type=MESH,
        )

    def arrival(p, dst, ssem, rsem):
        return pltpu.make_async_remote_copy(
            src_ref=dst.at[p], dst_ref=dst.at[p], send_sem=ssem.at[p], recv_sem=rsem.at[p],
            device_id=device(p), device_id_type=MESH,
        )

    loads = [
        pltpu.make_async_copy(src, dst, in_sem.at[i])
        for i, (src, dst) in enumerate(
            (
                (nb_hbm, nb), (before_hbm, before), (kind_hbm, kind), (quad_hbm, quad),
                (live_hbm, live), (mu_hbm, mu), (lam_hbm, lam), (level_hbm, level),
                (x_hbm, x), (twice_hbm, twice), (jac_hbm, jac), (inject_hbm, inject),
                (fill_hbm, fill), (unfill_hbm, unfill),
            )
        )
    ]
    for load in loads:
        load.start()
    barrier = pltpu.get_barrier_semaphore()
    for p in ORDER:
        if p != SELF:
            pl.semaphore_signal(barrier, inc=1, device_id=device(p), device_id_type=MESH)

    low_half = lane_iota((1, 128)) < 64

    loads[0].wait()
    loads[1].wait()
    tile_s[...] = jnp.zeros((8, 128), F32)
    want = nb[...]
    owner = want >> 6
    peer = ((owner >> 2) - me_m + 1) * 4 + ((owner - me_x) & 3)
    opposite = lax.broadcasted_iota(jnp.int32, (6, 64), 0) ^ 1
    tile_s[0:6, 0:64] = (peer * 512 + opposite * 64 + (want & 63)).astype(F32)
    packed = tile_s[...]
    turned = pltpu.roll(packed, 64, axis=1)
    pairs = [jnp.where(low_half, packed[f:f + 1], turned[f + 1:f + 2]) for f in (0, 2, 4)]
    row = jnp.concatenate(pairs, axis=1).astype(jnp.int32)
    peer_row = row >> 9
    ident = row & 511
    hits = lax.broadcasted_iota(jnp.int32, (16, ROWS), 0) == peer_row
    rank = dot(hits.astype(F32).astype(BF16), before[...])
    base = (lax.broadcasted_iota(jnp.int32, (16, ROWS), 0) * 64).astype(F32)
    slot = jnp.sum(jnp.where(hits, rank + base, 0.0), axis=0, keepdims=True)
    slot8 = jnp.broadcast_to(slot, (8, ROWS))
    place[...] = (
        lax.broadcasted_iota(jnp.int32, (SLOTS, ROWS), 0).astype(F32) == slot
    ).astype(F32).astype(BF16)
    which = lax.broadcasted_iota(jnp.int32, (8, ROWS), 0)
    parts = jnp.where(which == 0, ident & 63, jnp.where(which == 1, ident >> 6, 0)).astype(F32).astype(BF16)
    found = lax.dot_general(parts, place[...], (((1,), (1,)), ((), ())), preferred_element_type=F32)
    codes = found[0:1] + 64.0 * found[1:2]
    for t in range(6):
        lists[t] = jnp.broadcast_to(codes[:, 128 * t:128 * t + 128], (8, 128))

    pl.semaphore_wait(barrier, PEERS - 1)
    list_sends = [remote(p, lists.at[p // 2], lists_in, list_ssem, list_rsem) for p in ORDER if p != SELF]
    for send in list_sends:
        send.start()

    slot_col = slot8.T[:, 0:1]
    place_t[...] = (lane_iota((ROWS, SLOTS)).astype(F32) == slot_col).astype(F32).astype(BF16)

    for load in loads[2:8]:
        load.wait()
    scale = jnp.left_shift(jnp.ones((1, 64), jnp.int32), level[...]).astype(F32) * 0.25
    tile_s[...] = jnp.zeros((8, 128), F32)
    tile_s[0:1, 0:64] = lam[...] * scale * scale
    tile_s[1:2, 0:64] = mu[...] * scale * scale
    tile_s[2:3, 0:64] = live[...].astype(F32)
    flat = tile_s[...].T
    for i in range(3):
        coef[i] = jnp.broadcast_to(flat[0:64, i:i + 1], (64, 128))
    tile_s[...] = jnp.zeros((8, 128), F32)
    kinds = kind[...]
    tile_s[0:6, 0:64] = jnp.where(kinds == 1, 4, jnp.where(kinds == 2, quad[...], -1)).astype(F32)
    flat = tile_s[...].T
    for f in range(6):
        code_b[64 * f:64 * f + 64] = jnp.broadcast_to(flat[0:64, f:f + 1], (64, 128))

    loads[8].wait()
    alive = jnp.concatenate([coef[2]] * 4, axis=1)
    for c in range(3):
        x[c] = x[c] * alive
    loads[9].wait()
    for i, part in enumerate(split(x[...].reshape(192, 512))):
        layers = dot(part, twice[...])
        for f in range(6):
            cut = layers[:, 128 * f:128 * f + 128]
            table[i, 64 * f:64 * f + 64, 0:128] = jnp.where(low_half, cut[0:64], cut[64:128]).astype(BF16)
            table[i, 64 * f:64 * f + 64, 128:256] = cut[128:192].astype(BF16)

    def pack(buffer, p, rows):
        buffer[p, 0:64] = rows[:, 0:128]
        buffer[p, 64:96] = jnp.where(low_half, rows[0:32, 128:256], rows[32:64, 128:256])

    def unpack(message):
        tail = message[64:96]
        other = pltpu.roll(tail, 64, axis=1)
        third = jnp.concatenate(
            [jnp.where(low_half, tail, other), jnp.where(low_half, other, tail)], axis=0
        )
        return jnp.concatenate([message[0:64], third], axis=1)

    lane_row = lane_iota((64, ROWS)).astype(F32)
    lists_in[SELF] = lists[SELF // 2]
    f_sends = []
    for group in GROUPS:
        for n, p in enumerate(group):
            if p != SELF:
                arrival(p, lists_in, list_ssem, list_rsem).wait_recv()
            column = lists_in[p].T[64 * (p % 2):64 * (p % 2) + 64, 0:1]
            sel[64 * n:64 * n + 64] = (lane_row == column).astype(F32).astype(BF16)
        chosen = sel[0:64 * len(group)]
        rows = dot(chosen, table[0]) + dot(chosen, table[1])
        for n, p in enumerate(group):
            cut = rows[64 * n:64 * n + 64]
            if p == SELF:
                pack(frecv, p, cut)
            else:
                pack(fsend, p, cut)
                send = remote(p, fsend.at[p], frecv, f_ssem, f_rsem)
                send.start()
                f_sends.append(send)

    down_iota = lax.broadcasted_iota(jnp.int32, (ROWS, 128), 0).astype(F32)
    for t in range(6):
        ids = jnp.where(low_half, lists_in[2 * t], lists_in[2 * t + 1])[0:1]
        sel_t[:, 128 * t:128 * t + 128] = (down_iota == ids).astype(F32).astype(BF16)
    loads[10].wait()

    lane = lane_iota((1, 128))
    ok_up2, ok_dn2 = (lane & 7) < 7, (lane & 7) > 0
    ok_up1, ok_dn1 = (lane & 63) < 56, (lane & 63) >= 8

    def step2(v):
        return jnp.where(ok_up2, pltpu.roll(v, 127, axis=1), 0.0) - jnp.where(ok_dn2, pltpu.roll(v, 1, axis=1), 0.0)

    def step1(v):
        return jnp.where(ok_up1, pltpu.roll(v, 120, axis=1), 0.0) - jnp.where(ok_dn1, pltpu.roll(v, 8, axis=1), 0.0)

    def step0(tiles):
        swung = [pltpu.roll(v, 64, axis=1) for v in tiles]
        none = jnp.zeros_like(swung[0])
        up = [jnp.where(low_half, swung[t], swung[t + 1] if t < 3 else none) for t in range(4)]
        dn = [jnp.where(low_half, swung[t - 1] if t > 0 else none, swung[t]) for t in range(4)]
        return [u - d for u, d in zip(up, dn)]

    pair_of = {(0, 0): 0, (1, 1): 1, (2, 2): 2, (0, 1): 3, (0, 2): 4, (1, 2): 5}

    def pair(a, b):
        return pair_of[(min(a, b), max(a, b))]

    def inner(i, _):
        rows = pl.ds(pl.multiple_of(i * 8, 8), 8)
        tiles = [[x[c, rows, 128 * t:128 * t + 128] for t in range(4)] for c in range(3)]
        first = [step0(tiles[c]) for c in range(3)]
        for t in range(4):
            cols = slice(128 * t, 128 * t + 128)
            d = [[first[c][t], step1(tiles[c][t]), step2(tiles[c][t])] for c in range(3)]
            for a in range(3):
                sym[a, rows, cols] = d[a][a]
                for b in range(a + 1, 3):
                    sym[pair(a, b), rows, cols] = d[a][b] + d[b][a]
            jac[rows, cols] = coef[1, rows] - coef[0, rows] * jnp.log(jac[rows, cols])
        return 0

    lax.fori_loop(0, 8, inner, 0)

    for load in loads[11:14]:
        load.wait()

    raw = [jnp.zeros((ROWS, 256), F32), jnp.zeros((ROWS, 256), F32)]
    for p in ORDER:
        if p != SELF:
            arrival(p, frecv, f_ssem, f_rsem).wait_recv()
    for i, part in enumerate(split(jnp.concatenate([unpack(frecv[p]) for p in range(PEERS)], axis=0))):
        raw[i] = dot(place_t[...], part)
    code = code_b[...]
    raw_b = [r.astype(BF16) for r in raw]
    ghost = []
    for part in range(2):
        cut = slice(128 * part, 128 * part + 128)
        spread = dot(raw_b[0][:, cut], fill[...]) + dot(raw_b[1][:, cut], fill[...])
        value = jnp.where(code == 4.0, raw[0][:, cut] + raw[1][:, cut], 0.0)
        for q in range(4):
            value = jnp.where(code == float(q), spread[:, 128 * q:128 * q + 128], value)
        ghost.append(value)
    for a in range(3):
        low = [-g[128 * a:128 * a + 64] for g in ghost]
        high = [g[128 * a + 64:128 * a + 128] for g in ghost]
        sides = jnp.concatenate(
            [
                jnp.where(low_half, low[0], pltpu.roll(high[0], 64, axis=1)),
                jnp.where(low_half, pltpu.roll(low[0], 64, axis=1), high[0]),
                jnp.where(low_half, low[1], high[1]),
            ],
            axis=0,
        )
        h, l = split(sides)
        weights = inject[128 * a:128 * a + 128]
        inj[a] = (dot(h, weights) + dot(l, weights)).reshape(3, 64, 512)

    def stress(i, _):
        rows = pl.ds(pl.multiple_of(i * 8, 8), 8)
        for t in range(4):
            cols = slice(128 * t, 128 * t + 128)
            shear = jac[rows, cols]
            diag = [sym[a, rows, cols] + inj[a, a, rows, cols] for a in range(3)]
            trace = coef[0, rows] * (diag[0] + diag[1] + diag[2])
            for a in range(3):
                sym[a, rows, cols] = trace + 2.0 * shear * diag[a]
                for b in range(a + 1, 3):
                    both = sym[pair(a, b), rows, cols] + inj[a, b, rows, cols] + inj[b, a, rows, cols]
                    sym[pair(a, b), rows, cols] = shear * both
        return 0

    lax.fori_loop(0, 8, stress, 0)

    bars = [[None] * 6 for _ in range(2)]
    for a in range(3):
        stacked = jnp.concatenate([sym[pair(c, a)] for c in range(3)], axis=0)
        for i, part in enumerate(split(stacked)):
            layers = dot(part, twice[:, 256 * a:256 * a + 256])
            for side in range(2):
                cut = layers[:, 128 * side:128 * side + 128]
                if side == 0:
                    cut = -cut
                bars[i][2 * a + side] = jnp.concatenate(
                    [jnp.where(low_half, cut[0:64], cut[64:128]), cut[128:192]], axis=1
                )
    bar = [jnp.concatenate(b, axis=0) for b in bars]
    bar_b = [b.astype(BF16) for b in bar]
    leaving = []
    for part in range(2):
        cut = slice(128 * part, 128 * part + 128)
        spread = dot(bar_b[0][:, cut], unfill[...]) + dot(bar_b[1][:, cut], unfill[...])
        value = jnp.where(code == 4.0, bar[0][:, cut] + bar[1][:, cut], 0.0)
        for q in range(4):
            value = jnp.where(code == float(q), spread[:, 128 * q:128 * q + 128], value)
        leaving.append(value)
    h, l = split(jnp.concatenate(leaving, axis=1))
    a_sends = []
    for group in GROUPS:
        for p in group:
            chosen = place[64 * p:64 * p + 64]
            cut = dot(chosen, h) + dot(chosen, l)
            if p == SELF:
                pack(arecv, p, cut)
            else:
                pack(asend, p, cut)
                send = remote(p, asend.at[p], arecv, a_ssem, a_rsem)
                send.start()
                a_sends.append(send)

    def outer(i, _):
        rows = pl.ds(pl.multiple_of(i * 8, 8), 8)
        for c in range(3):
            first = step0([sym[pair(c, 0), rows, 128 * t:128 * t + 128] for t in range(4)])
            for t in range(4):
                cols = slice(128 * t, 128 * t + 128)
                back[c, rows, cols] = -(
                    first[t] + step1(sym[pair(c, 1), rows, cols]) + step2(sym[pair(c, 2), rows, cols])
                )
        return 0

    lax.fori_loop(0, 8, outer, 0)

    for p in ORDER:
        if p != SELF:
            arrival(p, arecv, a_ssem, a_rsem).wait_recv()
    h, l = split(jnp.concatenate([unpack(arecv[p]) for p in range(PEERS)], axis=0))
    landed_rows[...] = dot(sel_t[...], h) + dot(sel_t[...], l)
    total = jnp.zeros((192, 512), F32)
    for a in range(3):
        low = landed_rows[128 * a:128 * a + 64]
        high = landed_rows[128 * a + 64:128 * a + 128]
        sides = jnp.concatenate(
            [
                jnp.where(low_half, low[:, 0:128], pltpu.roll(high[:, 0:128], 64, axis=1)),
                jnp.where(low_half, pltpu.roll(low[:, 0:128], 64, axis=1), high[:, 0:128]),
                jnp.where(low_half, low[:, 128:256], high[:, 128:256]),
            ],
            axis=0,
        )
        h, l = split(sides)
        weights = inject[128 * a:128 * a + 128]
        total = total + dot(h, weights) + dot(l, weights)
    for c in range(3):
        out_ref[c] = (back[c] + total[64 * c:64 * c + 64]) * alive

    for send in list_sends + f_sends + a_sends:
        send.wait_send()


def per_device(
    direction, jacobian, shear_modulus, lame_modulus, refine_level, live_flag, neighbor, face_kind, face_quadrant
):
    ranges = lax.axis_size("morton")
    consts = tables()
    operands = [
        jnp.transpose(direction, (1, 0, 2)),
        jacobian,
        shear_modulus[None, :],
        lame_modulus[None, :],
        refine_level[None, :],
        live_flag[None, :],
        neighbor.T,
        face_kind.T,
        face_quadrant.T,
    ] + consts
    buffers = [pltpu.VMEM(o.shape, o.dtype) for o in operands]
    message = pltpu.VMEM((PEERS, 96, 128), F32)
    peers = pltpu.SemaphoreType.DMA((PEERS,))
    result = pl.pallas_call(
        functools.partial(kernel, ranges),
        out_shape=jax.ShapeDtypeStruct((3, BLOCKS, 512), F32),
        in_specs=[pl.BlockSpec(memory_space=pl.ANY)] * len(operands),
        out_specs=pl.BlockSpec(memory_space=pltpu.VMEM),
        scratch_shapes=buffers
        + [
            pltpu.VMEM((8, 128), F32),
            pltpu.VMEM((ROWS, 128), F32),
            pltpu.VMEM((3, 64, 128), F32),
            pltpu.VMEM((2, ROWS, 256), BF16),
            pltpu.VMEM((ROWS, ROWS), BF16),
            pltpu.VMEM((ROWS, SLOTS), BF16),
            pltpu.VMEM((SLOTS, ROWS), BF16),
            pltpu.VMEM((ROWS, SLOTS), BF16),
            pltpu.VMEM((6, 8, 128), F32),
            pltpu.VMEM((PEERS, 8, 128), F32),
            message,
            message,
            message,
            message,
            pltpu.VMEM((ROWS, 256), F32),
            pltpu.VMEM((6, 64, 512), F32),
            pltpu.VMEM((3, 3, 64, 512), F32),
            pltpu.VMEM((3, 64, 512), F32),
            pltpu.SemaphoreType.DMA((len(operands),)),
            peers,
            peers,
            peers,
            peers,
            peers,
            peers,
        ],
        compiler_params=pltpu.CompilerParams(
            collective_id=0, has_side_effects=True, vmem_limit_bytes=40 * 1024 * 1024
        ),
        name="hessian_exchange",
    )(*operands)
    return jnp.transpose(result, (1, 0, 2))


def solution(mesh):
    in_specs = (
        P(("morton", "sub"), None, None),
        P(("morton", "sub"), None),
        P(("morton", "sub")),
        P(("morton", "sub")),
        P(("morton", "sub")),
        P(("morton", "sub")),
        P(("morton", "sub"), None),
        P(("morton", "sub"), None),
        P(("morton", "sub"), None),
    )
    out_specs = P(("morton", "sub"), None, None)
    return jax.shard_map(
        per_device, mesh=mesh, in_specs=in_specs, out_specs=out_specs, check_vma=False
    )
```

time: 190 us -> 53.8 us (0.28)
  the two profiles are of different devices: /device:TPU:8 before, /device:TPU:1 now
where the time goes in v1:
time: 53.8 us; the launch traced here: 53.4 us
  Pallas kernels  45.1 us (84%)
  local copies, waits for them, and re-layouts  8.26 us (15%)
    pallas_call x1, Pallas kernels, per_device(): pl.pallas_call(functools.partial(kernel, ranges), out_shape=jax.ShapeDtyp...  45.1 us
    unnamed x29, local copies, waits for them, and re-layouts  8.26 us

profile of v1, /device:TPU:1, one launch (start us, length us, event | category | flops | bytes accessed | tf_op | source)
XLA Modules:
  0.0 53.4 jit_solution(856085621516445441)
XLA Ops:
  0.0 0.0 copy-start.12
  0.0 0.0 copy-start.13
  0.0 0.0 copy-start.9
  0.0 0.0 copy-start.8
  0.0 0.0 copy-start.7
  0.0 0.0 copy-start.10
  0.0 0.0 copy-start.11
  0.0 0.6 %copy-done.12 = s32[64]{0:T(128)S(1)} copy-done((s32[64]{0:T(128)S(1)}, s32[64]{0:T(128)}, u32[]{:S(2)}) %copy-start.12) | copy-done | bytes 280
  0.7 0.0 copy-done.13
  0.7 0.0 copy-done.9
  0.7 0.0 copy-done.8
  0.7 0.0 copy-done.7
  0.8 0.0 copy-done.10
  0.8 0.0 copy-done.11
  0.8 0.0 copy-start
  0.8 1.1 %copy-done = bf16[512,768]{1,0:T(8,128)(2,1)S(1)} copy-done((bf16[512,768]{1,0:T(8,128)(2,1)S(1)}, bf16[512,768]{1,0:T(8,128)(2,1)}, u32[]{:S(2)}) %copy-start) | copy-done | bytes 786456
  1.9 0.0 copy-start.1
  1.9 1.0 %copy-done.1 = f32[64,3,512]{2,0,1:T(8,128)S(1)} copy-done((f32[64,3,512]{2,0,1:T(8,128)S(1)}, f32[64,3,512]{2,0,1:T(8,128)}, u32[]{:S(2)}) %copy-start.1) | copy-done | bytes 393240
  2.9 0.0 copy-start.2
  2.9 1.0 %copy-done.2 = bf16[384,512]{1,0:T(8,128)(2,1)S(1)} copy-done((bf16[384,512]{1,0:T(8,128)(2,1)S(1)}, bf16[384,512]{1,0:T(8,128)(2,1)}, u32[]{:S(2)}) %copy-start.2) | copy-done | bytes 393240
  3.9 0.0 copy-start.3
  3.9 1.0 %copy-done.3 = bf16[384,384]{1,0:T(8,128)(2,1)S(1)} copy-done((bf16[384,384]{1,0:T(8,128)(2,1)S(1)}, bf16[384,384]{1,0:T(8,128)(2,1)}, u32[]{:S(2)}) %copy-start.3) | copy-done | bytes 294936
  4.8 0.0 copy-start.4
  4.8 0.9 %copy-done.4 = f32[64,512]{1,0:T(8,128)S(1)} copy-done((f32[64,512]{1,0:T(8,128)S(1)}, f32[64,512]{1,0:T(8,128)}, u32[]{:S(2)}) %copy-start.4) | copy-done | bytes 131096
  5.8 0.0 copy-start.5
  5.8 0.9 %copy-done.5 = bf16[128,512]{1,0:T(8,128)(2,1)S(1)} copy-done((bf16[128,512]{1,0:T(8,128)(2,1)S(1)}, bf16[128,512]{1,0:T(8,128)(2,1)}, u32[]{:S(2)}) %copy-start.5) | copy-done | bytes 131096
  6.7 0.0 copy-start.6
  6.7 0.9 %copy-done.6 = bf16[128,512]{1,0:T(8,128)(2,1)S(1)} copy-done((bf16[128,512]{1,0:T(8,128)(2,1)S(1)}, bf16[128,512]{1,0:T(8,128)(2,1)}, u32[]{:S(2)}) %copy-start.6) | copy-done | bytes 131096
  7.6 45.1 %hessian_exchange.1 = f32[3,64,512]{2,1,0:T(8,128)S(1)} custom-call(f32[3,64,512]{2,1,0:T(8,128)S(1)} %bitcast.10, f32[64,512]{1,0:T(8,128)S(1)} %copy-done.4, f32[1,64]{1,0:T(1,128)S(1)} %bitcast.14, f32[1,64]{1,0:T(1,128)S(1)} %bitcast.15, s32[1,64]{1,0:T(1,128)S(1)} %bitcast.16, s32[1,64]{1,0:T(1,128)S(1)} %bitcast.17, s32[6,64]{1,0:T(8,128)S(1)} %bitcast.11, ...), custom_call_target="tpu_custom_call" | custom-call | tf_op jit(solution)/shard_map/hessian_exchange/pallas_call | solution.py:407
  52.7 0.7 %copy.16 = f32[64,3,512]{2,0,1:T(8,128)} copy(f32[64,3,512]{2,0,1:T(8,128)S(1)} %bitcast.9) | data formatting | bytes 786432
Async XLA Ops:
  0.0 0.7 %copy-start.12 = (s32[64]{0:T(128)S(1)}, s32[64]{0:T(128)}, u32[]{:S(2)}) copy-start(s32[64]{0:T(128)} %param.18) | copy-start | bytes 772
  0.0 0.7 %copy-start.13 = (s32[64]{0:T(128)S(1)}, s32[64]{0:T(128)}, u32[]{:S(2)}) copy-start(s32[64]{0:T(128)} %param.19) | copy-start | bytes 772
  0.0 0.7 %copy-start.9 = (s32[64,6]{0,1:T(8,128)S(1)}, s32[64,6]{0,1:T(8,128)}, u32[]{:S(2)}) copy-start(s32[64,6]{0,1:T(8,128)} %param.22) | copy-start | bytes 4612
  0.0 0.7 %copy-start.8 = (s32[64,6]{0,1:T(8,128)S(1)}, s32[64,6]{0,1:T(8,128)}, u32[]{:S(2)}) copy-start(s32[64,6]{0,1:T(8,128)} %param.21) | copy-start | bytes 4612
  0.0 0.7 %copy-start.7 = (s32[64,6]{0,1:T(8,128)S(1)}, s32[64,6]{0,1:T(8,128)}, u32[]{:S(2)}) copy-start(s32[64,6]{0,1:T(8,128)} %param.20) | copy-start | bytes 4612
  0.0 0.7 %copy-start.10 = (f32[64]{0:T(128)S(1)}, f32[64]{0:T(128)}, u32[]{:S(2)}) copy-start(f32[64]{0:T(128)} %param.16) | copy-start | bytes 772
  0.0 0.7 %copy-start.11 = (f32[64]{0:T(128)S(1)}, f32[64]{0:T(128)}, u32[]{:S(2)}) copy-start(f32[64]{0:T(128)} %param.17) | copy-start | bytes 772
  0.8 1.1 %copy-start = (bf16[512,768]{1,0:T(8,128)(2,1)S(1)}, bf16[512,768]{1,0:T(8,128)(2,1)}, u32[]{:S(2)}) copy-start(bf16[512,768]{1,0:T(8,128)(2,1)} %constant.10.clone.twice_hbm) | copy-start | bytes 2359300
  1.9 1.0 %copy-start.1 = (f32[64,3,512]{2,0,1:T(8,128)S(1)}, f32[64,3,512]{2,0,1:T(8,128)}, u32[]{:S(2)}) copy-start(f32[64,3,512]{2,0,1:T(8,128)} %param.14) | copy-start | bytes 1179652
  2.9 1.0 %copy-start.2 = (bf16[384,512]{1,0:T(8,128)(2,1)S(1)}, bf16[384,512]{1,0:T(8,128)(2,1)}, u32[]{:S(2)}) copy-start(bf16[384,512]{1,0:T(8,128)(2,1)} %constant.11.clone.inject_hbm) | copy-start | bytes 1179652
  3.9 1.0 %copy-start.3 = (bf16[384,384]{1,0:T(8,128)(2,1)S(1)}, bf16[384,384]{1,0:T(8,128)(2,1)}, u32[]{:S(2)}) copy-start(bf16[384,384]{1,0:T(8,128)(2,1)} %constant.14.clone.before_hbm) | copy-start | bytes 884740
  4.8 0.9 %copy-start.4 = (f32[64,512]{1,0:T(8,128)S(1)}, f32[64,512]{1,0:T(8,128)}, u32[]{:S(2)}) copy-start(f32[64,512]{1,0:T(8,128)} %jac_hbm.1) | copy-start | bytes 393220
  5.8 0.9 %copy-start.5 = (bf16[128,512]{1,0:T(8,128)(2,1)S(1)}, bf16[128,512]{1,0:T(8,128)(2,1)}, u32[]{:S(2)}) copy-start(bf16[128,512]{1,0:T(8,128)(2,1)} %constant.13.clone.unfill_hbm) | copy-start | bytes 393220
  6.7 0.9 %copy-start.6 = (bf16[128,512]{1,0:T(8,128)(2,1)S(1)}, bf16[128,512]{1,0:T(8,128)(2,1)}, u32[]{:S(2)}) copy-start(bf16[128,512]{1,0:T(8,128)(2,1)} %constant.12.clone.fill_hbm) | copy-start | bytes 393220

commit v2 on v1

--- a/solution.py
+++ b/solution.py
@@ -18,6 +18,7 @@
 MESH = pl.DeviceIdType.MESH
 GROUPS = ((2, 6, 10), (1, 3, 5, 7, 9, 11), (0, 8, 4))
 ORDER = tuple(p for group in GROUPS for p in group)
+OTHERS = tuple(p for p in ORDER if p != SELF)
 
 
 def tables():
@@ -77,9 +78,19 @@
     me_m = lax.axis_index("morton")
     me_x = lax.axis_index("sub")
 
+    has_low = me_m > 0
+    has_high = me_m < ranges - 1
+    present = 3 + 4 * has_low.astype(jnp.int32) + 4 * has_high.astype(jnp.int32)
+
     def device(p):
-        dm, dx = p // 4 - 1, p % 4
-        return (lax.rem(me_m + (dm + ranges), ranges), lax.rem(me_x + dx, 4))
+        return (me_m + (p // 4 - 1), lax.rem(me_x + p % 4, 4))
+
+    def guarded(p, act):
+        if p // 4 == 1:
+            act()
+        else:
+            pl.when(has_low if p // 4 == 0 else has_high)(act)
+
 
     def mirror(p):
         return (2 - p // 4) * 4 + (4 - p % 4) % 4
@@ -110,11 +121,18 @@
     for load in loads:
         load.start()
     barrier = pltpu.get_barrier_semaphore()
-    for p in ORDER:
-        if p != SELF:
-            pl.semaphore_signal(barrier, inc=1, device_id=device(p), device_id_type=MESH)
+    for p in OTHERS:
+        guarded(p, lambda p=p: pl.semaphore_signal(barrier, inc=1, device_id=device(p), device_id_type=MESH))
 
     low_half = lane_iota((1, 128)) < 64
+
+    def clear(first):
+        for buffer in (frecv, arecv):
+            buffer[first:first + 4] = jnp.zeros((4, 96, 128), F32)
+        lists_in[first:first + 4] = jnp.zeros((4, 8, 128), F32)
+
+    pl.when(jnp.logical_not(has_low))(lambda: clear(0))
+    pl.when(jnp.logical_not(has_high))(lambda: clear(8))
 
     loads[0].wait()
     loads[1].wait()
@@ -145,10 +163,18 @@
     for t in range(6):
         lists[t] = jnp.broadcast_to(codes[:, 128 * t:128 * t + 128], (8, 128))
 
-    pl.semaphore_wait(barrier, PEERS - 1)
-    list_sends = [remote(p, lists.at[p // 2], lists_in, list_ssem, list_rsem) for p in ORDER if p != SELF]
-    for send in list_sends:
-        send.start()
+    pl.semaphore_wait(barrier, present)
+    sends = []
+
+    def start(send, p):
+        guarded(p, send.start)
+        sends.append((p, send))
+
+    def await_rows(p, dst, ssem, rsem):
+        guarded(p, arrival(p, dst, ssem, rsem).wait_recv)
+
+    for p in OTHERS:
+        start(remote(p, lists.at[p // 2], lists_in, list_ssem, list_rsem), p)
 
     slot_col = slot8.T[:, 0:1]
     place_t[...] = (lane_iota((ROWS, SLOTS)).astype(F32) == slot_col).astype(F32).astype(BF16)
@@ -196,11 +222,10 @@
 
     lane_row = lane_iota((64, ROWS)).astype(F32)
     lists_in[SELF] = lists[SELF // 2]
-    f_sends = []
     for group in GROUPS:
         for n, p in enumerate(group):
             if p != SELF:
-                arrival(p, lists_in, list_ssem, list_rsem).wait_recv()
+                await_rows(p, lists_in, list_ssem, list_rsem)
             column = lists_in[p].T[64 * (p % 2):64 * (p % 2) + 64, 0:1]
             sel[64 * n:64 * n + 64] = (lane_row == column).astype(F32).astype(BF16)
         chosen = sel[0:64 * len(group)]
@@ -211,9 +236,7 @@
                 pack(frecv, p, cut)
             else:
                 pack(fsend, p, cut)
-                send = remote(p, fsend.at[p], frecv, f_ssem, f_rsem)
-                send.start()
-                f_sends.append(send)
+                start(remote(p, fsend.at[p], frecv, f_ssem, f_rsem), p)
 
     down_iota = lax.broadcasted_iota(jnp.int32, (ROWS, 128), 0).astype(F32)
     for t in range(6):
@@ -263,9 +286,8 @@
         load.wait()
 
     raw = [jnp.zeros((ROWS, 256), F32), jnp.zeros((ROWS, 256), F32)]
-    for p in ORDER:
-        if p != SELF:
-            arrival(p, frecv, f_ssem, f_rsem).wait_recv()
+    for p in OTHERS:
+        await_rows(p, frecv, f_ssem, f_rsem)
     for i, part in enumerate(split(jnp.concatenate([unpack(frecv[p]) for p in range(PEERS)], axis=0))):
         raw[i] = dot(place_t[...], part)
     code = code_b[...]
@@ -332,7 +354,6 @@
             value = jnp.where(code == float(q), spread[:, 128 * q:128 * q + 128], value)
         leaving.append(value)
     h, l = split(jnp.concatenate(leaving, axis=1))
-    a_sends = []
     for group in GROUPS:
         for p in group:
             chosen = place[64 * p:64 * p + 64]
@@ -341,9 +362,7 @@
                 pack(arecv, p, cut)
             else:
                 pack(asend, p, cut)
-                send = remote(p, asend.at[p], arecv, a_ssem, a_rsem)
-                send.start()
-                a_sends.append(send)
+                start(remote(p, asend.at[p], arecv, a_ssem, a_rsem), p)
 
     def outer(i, _):
         rows = pl.ds(pl.multiple_of(i * 8, 8), 8)
@@ -358,9 +377,8 @@
 
     lax.fori_loop(0, 8, outer, 0)
 
-    for p in ORDER:
-        if p != SELF:
-            arrival(p, arecv, a_ssem, a_rsem).wait_recv()
+    for p in OTHERS:
+        await_rows(p, arecv, a_ssem, a_rsem)
     h, l = split(jnp.concatenate([unpack(arecv[p]) for p in range(PEERS)], axis=0))
     landed_rows[...] = dot(sel_t[...], h) + dot(sel_t[...], l)
     total = jnp.zeros((192, 512), F32)
@@ -381,8 +399,8 @@
     for c in range(3):
         out_ref[c] = (back[c] + total[64 * c:64 * c + 64]) * alive
 
-    for send in list_sends + f_sends + a_sends:
-        send.wait_send()
+    for p, send in sends:
+        guarded(p, send.wait_send)
 
 
 def per_device(
@@ -402,12 +420,13 @@
         face_quadrant.T,
     ] + consts
     buffers = [pltpu.VMEM(o.shape, o.dtype) for o in operands]
+    operands = [pltpu.with_memory_space_constraint(o, pltpu.HBM) for o in operands]
     message = pltpu.VMEM((PEERS, 96, 128), F32)
     peers = pltpu.SemaphoreType.DMA((PEERS,))
     result = pl.pallas_call(
         functools.partial(kernel, ranges),
         out_shape=jax.ShapeDtypeStruct((3, BLOCKS, 512), F32),
-        in_specs=[pl.BlockSpec(memory_space=pl.ANY)] * len(operands),
+        in_specs=[pl.BlockSpec(memory_space=pltpu.HBM)] * len(operands),
         out_specs=pl.BlockSpec(memory_space=pltpu.VMEM),
         scratch_shapes=buffers
         + [
@@ -438,7 +457,7 @@
             peers,
         ],
         compiler_params=pltpu.CompilerParams(
-            collective_id=0, has_side_effects=True, vmem_limit_bytes=40 * 1024 * 1024
+            collective_id=0, has_side_effects=True, vmem_limit_bytes=48 * 1024 * 1024
         ),
         name="hessian_exchange",
     )(*operands)

time: 53.8 us -> 41.8 us (0.78)
  the two profiles are of different devices: /device:TPU:1 before, /device:TPU:49 now
where the time goes in v2:
time: 41.8 us; the launch traced here: 41.6 us
  Pallas kernels  40.9 us (98%)
  local copies, waits for them, and re-layouts  0.75 us (2%)
    pallas_call x1, Pallas kernels, per_device(): pl.pallas_call(functools.partial(kernel, ranges), out_shape=jax.ShapeDtyp...  40.9 us

profile of v2, /device:TPU:49, one launch (start us, length us, event | category | flops | bytes accessed | tf_op | source)
XLA Modules:
  0.0 41.6 jit_solution(4693214379471697934)
XLA Ops:
  0.0 40.9 %hessian_exchange.1 = f32[3,64,512]{2,1,0:T(8,128)S(1)} custom-call(f32[3,64,512]{2,1,0:T(8,128)} %bitcast.10, f32[64,512]{1,0:T(8,128)} %jac_hbm.1, f32[1,64]{1,0:T(1,128)} %bitcast.14, f32[1,64]{1,0:T(1,128)} %bitcast.15, s32[1,64]{1,0:T(1,128)} %bitcast.16, s32[1,64]{1,0:T(1,128)} %bitcast.17, s32[6,64]{1,0:T(8,128)} %bitcast.11, s32[6,64]{1,0:T(8,128)} %bitcast.12, ...), custom_call_target="tpu_custom_call" | custom-call | tf_op jit(solution)/shard_map/hessian_exchange/pallas_call | solution.py:426
  40.9 0.7 %copy.16 = f32[64,3,512]{2,0,1:T(8,128)} copy(f32[64,3,512]{2,0,1:T(8,128)S(1)} %bitcast.9) | data formatting | bytes 786432

commit v3 on v2

v3 whole, which is shorter than its diff:
```python
import functools

import jax
import jax.numpy as jnp
import numpy as np
from jax import lax
from jax.experimental import pallas as pl
from jax.experimental.pallas import tpu as pltpu
from jax.sharding import PartitionSpec as P

BLOCKS = 64
ROWS = 6 * BLOCKS
PEERS = 12
SLOTS = PEERS * BLOCKS
F32 = jnp.float32
BF16 = jnp.bfloat16
MESH = pl.DeviceIdType.MESH
STEPS = (1, 3, 2, 0)
SELF = 10
OTHERS = (6, 8, 7, 0, 2, 3, 5, 1, 4, 9, 11)
ARRIVALS = (3, 2, 0, 1)
PAIRS = {(0, 0): 0, (1, 1): 1, (2, 2): 2, (0, 1): 3, (0, 2): 4, (1, 2): 5}


def pair(a, b):
    return PAIRS[(min(a, b), max(a, b))]


def mirror(q):
    return 3 * STEPS.index((4 - STEPS[q // 3]) % 4) + 2 - q % 3


def tables():
    node = np.arange(512)
    coords = (node // 64, (node // 8) % 8, node % 8)
    pick = np.zeros((512, 6, 64), np.float32)
    for face in range(6):
        axis = face // 2
        others = [coords[a] for a in range(3) if a != axis]
        for n in np.nonzero(coords[axis] == 7 * (face % 2))[0]:
            pick[n, face, others[0][n] * 8 + others[1][n]] = 1
    halves = np.zeros((2, 8, 8), np.float32)
    for u in range(2):
        for i in range(8):
            halves[u, i, (7 * u + i) // 2] += 0.5
            halves[u, i, (7 * u + i + 1) // 2] += 0.5
    fill = np.zeros((128, 512), np.float32)
    unfill = np.zeros((128, 512), np.float32)
    for q in range(4):
        spread = np.kron(halves[q // 2], halves[q % 2])
        for half in range(2):
            lanes = slice(64 * half, 64 * half + 64)
            cols = slice(128 * q + 64 * half, 128 * q + 64 * half + 64)
            fill[lanes, cols] = spread.T
            unfill[lanes, cols] = spread
    twice = np.concatenate([pick, pick], axis=2).reshape(512, 768)
    inject = pick.reshape(512, 3, 128).transpose(1, 2, 0)
    inject = np.concatenate([inject, inject], axis=1).reshape(768, 512)
    before = np.triu(np.ones((ROWS, ROWS), np.float32), 1)
    stacked = (np.concatenate([t, t], axis=0) for t in (fill, unfill))
    return [jnp.asarray(t, BF16) for t in (twice, inject, *stacked, before)]


def split(values, axis):
    high = values.astype(BF16)
    low = (values - high.astype(F32)).astype(BF16)
    return jnp.concatenate([high, low], axis=axis)


def dot(a, b):
    return jnp.dot(a, b, preferred_element_type=F32)


def lane_iota(shape):
    return lax.broadcasted_iota(jnp.int32, shape, len(shape) - 1)


def row_iota(shape):
    return lax.broadcasted_iota(jnp.int32, shape, 0)


def one_hot(hits):
    return hits.astype(F32).astype(BF16)


def kernel(
    ranges,
    x_hbm, jac_hbm, mu_hbm, lam_hbm, level_hbm, live_hbm, nb_hbm, kind_hbm, quad_hbm,
    twice_hbm, inject_hbm, fill_hbm, unfill_hbm, before_hbm,
    out_ref,
    x, jac, mu, lam, level, live, nb, kind, quad,
    twice, inject, fill, unfill, before,
    tile_s, code_b, coef, table, sel_t, place, place_t, lists, lists_in,
    fsend, frecv, asend, arecv, gathered, leaving, sym, inj, back,
    in_sem, list_ssem, list_rsem, f_ssem, f_rsem, a_ssem, a_rsem,
):
    me_m = lax.axis_index("morton")
    me_x = lax.axis_index("sub")
    has_low = me_m > 0
    has_high = me_m < ranges - 1
    present = 3 + 4 * has_low.astype(jnp.int32) + 4 * has_high.astype(jnp.int32)
    low_half = lane_iota((1, 128)) < 64

    def device(q):
        return (me_m + (q % 3 - 1), lax.rem(me_x + STEPS[q // 3], 4))

    def guarded(q, act):
        if q % 3 == 1:
            act()
        else:
            pl.when(has_low if q % 3 == 0 else has_high)(act)

    sends = []

    def send(q, src, dst, ssem, rsem):
        copy = pltpu.make_async_remote_copy(
            src_ref=src.at[q], dst_ref=dst.at[mirror(q)], send_sem=ssem.at[q], recv_sem=rsem.at[mirror(q)],
            device_id=device(q), device_id_type=MESH,
        )
        guarded(q, copy.start)
        sends.append((q, copy))

    def arrive(q, dst, ssem, rsem):
        copy = pltpu.make_async_remote_copy(
            src_ref=dst.at[q], dst_ref=dst.at[q], send_sem=ssem.at[q], recv_sem=rsem.at[q],
            device_id=device(q), device_id_type=MESH,
        )
        guarded(q, copy.wait_recv)

    loads = [
        pltpu.make_async_copy(src, dst, in_sem.at[i])
        for i, (src, dst) in enumerate(
            (
                (nb_hbm, nb), (before_hbm, before), (kind_hbm, kind), (quad_hbm, quad),
                (live_hbm, live), (mu_hbm, mu), (lam_hbm, lam), (level_hbm, level),
                (x_hbm, x), (twice_hbm, twice), (jac_hbm, jac), (inject_hbm, inject),
                (fill_hbm, fill), (unfill_hbm, unfill),
            )
        )
    ]

    def loaded(first, last):
        for load in loads[first:last]:
            load.wait()

    def clear(first):
        for q in range(first, PEERS, 3):
            frecv[q] = jnp.zeros((96, 128), F32)
            arecv[q] = jnp.zeros((96, 128), F32)
            lists_in[q] = jnp.zeros((8, 128), F32)

    def request():
        loaded(0, 2)
        tile_s[...] = jnp.zeros((8, 128), F32)
        want = nb[...]
        owner = want >> 6
        step = (owner - me_x) & 3
        group = jnp.where(step == 1, 0, jnp.where(step == 3, 1, jnp.where(step == 2, 2, 3)))
        peer = group * 3 + ((owner >> 2) - me_m + 1)
        opposite = row_iota((6, 64)) ^ 1
        tile_s[0:6, 0:64] = (peer * 512 + opposite * 64 + (want & 63)).astype(F32)
        packed = tile_s[...]
        turned = pltpu.roll(packed, 64, axis=1)
        pairs = [jnp.where(low_half, packed[f:f + 1], turned[f + 1:f + 2]) for f in (0, 2, 4)]
        row = jnp.concatenate(pairs, axis=1).astype(jnp.int32)
        ident = row & 511
        hits = row_iota((16, ROWS)) == (row >> 9)
        rank = dot(one_hot(hits), before[...])
        base = (row_iota((16, ROWS)) * 64).astype(F32)
        slot = jnp.sum(jnp.where(hits, rank + base, 0.0), axis=0, keepdims=True)
        place[...] = one_hot(row_iota((SLOTS, ROWS)).astype(F32) == slot)
        which = row_iota((8, ROWS))
        parts = jnp.where(which == 0, ident & 63, jnp.where(which == 1, ident >> 6, 0))
        found = lax.dot_general(
            parts.astype(F32).astype(BF16), place[...], (((1,), (1,)), ((), ())), preferred_element_type=F32
        )
        codes = jnp.broadcast_to(found[0:1] + 64.0 * found[1:2], (8, SLOTS))
        for t in range(PEERS // 2):
            both = codes[:, 128 * t:128 * t + 128]
            swapped = pltpu.roll(both, 64, axis=1)
            lists[2 * t] = jnp.where(low_half, both, swapped)
            lists[2 * t + 1] = jnp.where(low_half, swapped, both)
        return slot

    def prepare(slot):
        slot_col = jnp.broadcast_to(slot, (8, ROWS)).T[:, 0:1]
        lanes = lane_iota((ROWS, ROWS))
        lanes = jnp.where(lanes < 192, lanes, lanes - 192).astype(F32)
        for i in range(4):
            place_t[i] = one_hot(lanes == slot_col - 192.0 * i)
        loaded(2, 8)
        scale = jnp.left_shift(jnp.ones((1, 64), jnp.int32), level[...]).astype(F32) * 0.25
        tile_s[...] = jnp.zeros((8, 128), F32)
        tile_s[0:1, 0:64] = lam[...] * scale * scale
        tile_s[1:2, 0:64] = mu[...] * scale * scale
        tile_s[2:3, 0:64] = live[...].astype(F32)
        flat = tile_s[...].T
        for i in range(3):
            coef[i] = jnp.broadcast_to(flat[0:64, i:i + 1], (64, 128))
        tile_s[...] = jnp.zeros((8, 128), F32)
        kinds = kind[...]
        tile_s[0:6, 0:64] = jnp.where(kinds == 1, 4, jnp.where(kinds == 2, quad[...], -1)).astype(F32)
        flat = tile_s[...].T
        for f in range(6):
            code_b[64 * f:64 * f + 64] = jnp.broadcast_to(flat[0:64, f:f + 1], (64, 128))
        loaded(8, 9)
        alive = jnp.concatenate([coef[2]] * 4, axis=1)
        for c in range(3):
            x[c] = x[c] * alive
        loaded(9, 10)
        parts = split(x[...].reshape(192, 512), 0)
        layers = dot(parts, twice[...])
        for i in range(2):
            for f in range(6):
                cut = layers[192 * i:192 * i + 192, 128 * f:128 * f + 128]
                rows = slice(ROWS * i + 64 * f, ROWS * i + 64 * f + 64)
                table[rows, 0:128] = jnp.where(low_half, cut[0:64], cut[64:128]).astype(BF16)
                table[rows, 128:256] = cut[128:192].astype(BF16)

    def pack(buffer, q, rows):
        buffer[q, 0:64] = rows[:, 0:128]
        buffer[q, 64:96] = jnp.where(low_half, rows[0:32, 128:256], rows[32:64, 128:256])

    def unpack(message):
        tail = message[64:96]
        other = pltpu.roll(tail, 64, axis=1)
        third = jnp.concatenate([jnp.where(low_half, tail, other), jnp.where(low_half, other, tail)], axis=0)
        return jnp.concatenate([message[0:64], third], axis=1)

    def gather(i):
        lane_row = lane_iota((64, ROWS)).astype(F32)
        chosen = []
        for q in range(3 * i, 3 * i + 3):
            column = lists_in[q].T[0:64, 0:1]
            chosen.append(one_hot(lane_row == column))
        chosen = jnp.concatenate(chosen, axis=0)
        rows = dot(jnp.concatenate([chosen, chosen], axis=1), table[...])
        for n in range(3):
            q = 3 * i + n
            pack(frecv if q == SELF else fsend, q, rows[64 * n:64 * n + 64])

    def selection(i):
        a, b, c = (lists_in[q][0:1] for q in range(3 * i, 3 * i + 3))
        ids = [jnp.where(low_half, u, v) for u, v in ((a, b), (c, a), (b, c))]
        sel_t[i] = one_hot(row_iota((ROWS, ROWS)).astype(F32) == jnp.concatenate(ids, axis=1))

    def collect(i, weights, messages, first):
        rows = jnp.concatenate([unpack(messages[q]) for q in range(3 * i, 3 * i + 3)], axis=0)
        part = dot(weights[i], split(rows, 0))
        gathered[...] = part if first else gathered[...] + part

    lane = lane_iota((1, 128))
    ok_up2, ok_dn2 = (lane & 7) < 7, (lane & 7) > 0
    ok_up1, ok_dn1 = (lane & 63) < 56, (lane & 63) >= 8

    def step2(v):
        return jnp.where(ok_up2, pltpu.roll(v, 127, axis=1), 0.0) - jnp.where(ok_dn2, pltpu.roll(v, 1, axis=1), 0.0)

    def step1(v):
        return jnp.where(ok_up1, pltpu.roll(v, 120, axis=1), 0.0) - jnp.where(ok_dn1, pltpu.roll(v, 8, axis=1), 0.0)

    def step0(tiles):
        swung = [pltpu.roll(v, 64, axis=1) for v in tiles]
        none = jnp.zeros_like(swung[0])
        up = [jnp.where(low_half, swung[t], swung[t + 1] if t < 3 else none) for t in range(4)]
        dn = [jnp.where(low_half, swung[t - 1] if t > 0 else none, swung[t]) for t in range(4)]
        return [u - d for u, d in zip(up, dn)]

    def inner(i, _):
        rows = pl.ds(pl.multiple_of(i * 8, 8), 8)
        tiles = [[x[c, rows, 128 * t:128 * t + 128] for t in range(4)] for c in range(3)]
        first = [step0(tiles[c]) for c in range(3)]
        for t in range(4):
            cols = slice(128 * t, 128 * t + 128)
            d = [[first[c][t], step1(tiles[c][t]), step2(tiles[c][t])] for c in range(3)]
            for a in range(3):
                sym[a, rows, cols] = d[a][a]
                for b in range(a + 1, 3):
                    sym[pair(a, b), rows, cols] = d[a][b] + d[b][a]
            jac[rows, cols] = coef[1, rows] - coef[0, rows] * jnp.log(jac[rows, cols])
        return 0

    def by_quadrant(parts, weights):
        code = code_b[...]
        masks = [code == float(q) for q in range(5)]
        result = []
        for half in range(2):
            cut = slice(128 * half, 128 * half + 128)
            value = parts[:, cut]
            spread = dot(split(value, 1), weights[...])
            value = jnp.where(masks[4], value, 0.0)
            for q in range(4):
                value = jnp.where(masks[q], spread[:, 128 * q:128 * q + 128], value)
            result.append(value)
        return result

    def sided(parts, a, sign):
        low = [sign * part[128 * a:128 * a + 64] for part in parts]
        high = [part[128 * a + 64:128 * a + 128] for part in parts]
        return jnp.concatenate(
            [
                jnp.where(low_half, low[0], pltpu.roll(high[0], 64, axis=1)),
                jnp.where(low_half, pltpu.roll(low[0], 64, axis=1), high[0]),
                jnp.where(low_half, low[1], high[1]),
            ],
            axis=0,
        )

    def ghosts():
        parts = by_quadrant(gathered[...], fill)
        for a in range(3):
            sides = split(sided(parts, a, -1.0), 1)
            inj[a] = dot(sides, inject[256 * a:256 * a + 256]).reshape(3, 64, 512)

    def stress(i, _):
        rows = pl.ds(pl.multiple_of(i * 8, 8), 8)
        for t in range(4):
            cols = slice(128 * t, 128 * t + 128)
            shear = jac[rows, cols]
            diag = [sym[a, rows, cols] + inj[a, a, rows, cols] for a in range(3)]
            trace = coef[0, rows] * (diag[0] + diag[1] + diag[2])
            for a in range(3):
                sym[a, rows, cols] = trace + 2.0 * shear * diag[a]
                for b in range(a + 1, 3):
                    both = sym[pair(a, b), rows, cols] + inj[a, b, rows, cols] + inj[b, a, rows, cols]
                    sym[pair(a, b), rows, cols] = shear * both
        return 0

    def adjoint_faces():
        bars = []
        for a in range(3):
            stacked = jnp.concatenate([sym[pair(c, a)] for c in range(3)], axis=0)
            weights = twice[:, 256 * a:256 * a + 256]
            layers = dot(split(stacked, 1), jnp.concatenate([weights, weights], axis=0))
            for side in range(2):
                cut = layers[:, 128 * side:128 * side + 128]
                if side == 0:
                    cut = -cut
                bars.append(jnp.concatenate([jnp.where(low_half, cut[0:64], cut[64:128]), cut[128:192]], axis=1))
        parts = by_quadrant(jnp.concatenate(bars, axis=0), unfill)
        leaving[...] = split(jnp.concatenate(parts, axis=1), 0)

    def scatter(i):
        chosen = place[192 * i:192 * i + 192]
        rows = dot(jnp.concatenate([chosen, chosen], axis=1), leaving[...])
        for n in range(3):
            q = 3 * i + n
            pack(arecv if q == SELF else asend, q, rows[64 * n:64 * n + 64])

    def outer(i, _):
        rows = pl.ds(pl.multiple_of(i * 8, 8), 8)
        for c in range(3):
            first = step0([sym[pair(c, 0), rows, 128 * t:128 * t + 128] for t in range(4)])
            for t in range(4):
                cols = slice(128 * t, 128 * t + 128)
                back[c, rows, cols] = -(
                    first[t] + step1(sym[pair(c, 1), rows, cols]) + step2(sym[pair(c, 2), rows, cols])
                )
        return 0

    def land():
        rows = gathered[...]
        parts = [rows[:, 0:128], rows[:, 128:256]]
        sides = jnp.concatenate([split(sided(parts, a, 1.0), 1) for a in range(3)], axis=1)
        total = dot(sides, inject[...])
        alive = jnp.concatenate([coef[2]] * 4, axis=1)
        for c in range(3):
            out_ref[c] = (back[c] + total[64 * c:64 * c + 64]) * alive

    for load in loads:
        load.start()
    barrier = pltpu.get_barrier_semaphore()
    for q in OTHERS:
        guarded(q, lambda q=q: pl.semaphore_signal(barrier, inc=1, device_id=device(q), device_id_type=MESH))
    pl.when(jnp.logical_not(has_low))(lambda: clear(0))
    pl.when(jnp.logical_not(has_high))(lambda: clear(2))
    slot = request()
    pl.semaphore_wait(barrier, present)
    for q in OTHERS:
        send(q, lists, lists_in, list_ssem, list_rsem)
    lists_in[SELF] = lists[SELF]
    prepare(slot)

    for i in (2, 0, 1, 3):
        for q in range(3 * i, 3 * i + 3):
            if q != SELF:
                arrive(q, lists_in, list_ssem, list_rsem)
        gather(i)
        for q in range(3 * i, 3 * i + 3):
            if q != SELF:
                send(q, fsend, frecv, f_ssem, f_rsem)

    loaded(10, 11)
    lax.fori_loop(0, 8, inner, 0)
    for i in range(4):
        selection(i)
    loaded(11, 14)
    for n, i in enumerate(ARRIVALS):
        for q in range(3 * i, 3 * i + 3):
            if q != SELF:
                arrive(q, frecv, f_ssem, f_rsem)
        collect(i, place_t, frecv, n == 0)
    ghosts()
    lax.fori_loop(0, 8, stress, 0)
    adjoint_faces()
    for i in (2, 0, 1, 3):
        scatter(i)
        for q in range(3 * i, 3 * i + 3):
            if q != SELF:
                send(q, asend, arecv, a_ssem, a_rsem)

    lax.fori_loop(0, 8, outer, 0)
    for n, i in enumerate(ARRIVALS):
        for q in range(3 * i, 3 * i + 3):
            if q != SELF:
                arrive(q, arecv, a_ssem, a_rsem)
        collect(i, sel_t, arecv, n == 0)
    land()
    for q, copy in sends:
        guarded(q, copy.wait_send)


def per_device(
    direction, jacobian, shear_modulus, lame_modulus, refine_level, live_flag, neighbor, face_kind, face_quadrant
):
    ranges = lax.axis_size("morton")
    operands = [
        jnp.transpose(direction, (1, 0, 2)),
        jacobian,
        shear_modulus[None, :],
        lame_modulus[None, :],
        refine_level[None, :],
        live_flag[None, :],
        neighbor.T,
        face_kind.T,
        face_quadrant.T,
    ] + tables()
    buffers = [pltpu.VMEM(o.shape, o.dtype) for o in operands]
    operands = [pltpu.with_memory_space_constraint(o, pltpu.HBM) for o in operands]
    message = pltpu.VMEM((PEERS, 96, 128), F32)
    short = pltpu.VMEM((PEERS, 8, 128), F32)
    peers = pltpu.SemaphoreType.DMA((PEERS,))
    result = pl.pallas_call(
        functools.partial(kernel, ranges),
        out_shape=jax.ShapeDtypeStruct((3, BLOCKS, 512), F32),
        in_specs=[pl.BlockSpec(memory_space=pltpu.HBM)] * len(operands),
        out_specs=pl.BlockSpec(memory_space=pltpu.VMEM),
        scratch_shapes=buffers
        + [
            pltpu.VMEM((8, 128), F32),
            pltpu.VMEM((ROWS, 128), F32),
            pltpu.VMEM((3, 64, 128), F32),
            pltpu.VMEM((2 * ROWS, 256), BF16),
            pltpu.VMEM((4, ROWS, ROWS), BF16),
            pltpu.VMEM((SLOTS, ROWS), BF16),
            pltpu.VMEM((4, ROWS, ROWS), BF16),
            short,
            short,
            message,
            message,
            message,
            message,
            pltpu.VMEM((ROWS, 256), F32),
            pltpu.VMEM((2 * ROWS, 256), BF16),
            pltpu.VMEM((6, 64, 512), F32),
            pltpu.VMEM((3, 3, 64, 512), F32),
            pltpu.VMEM((3, 64, 512), F32),
            pltpu.SemaphoreType.DMA((len(operands),)),
            peers,
            peers,
            peers,
            peers,
            peers,
            peers,
        ],
        compiler_params=pltpu.CompilerParams(
            collective_id=0, has_side_effects=True, vmem_limit_bytes=48 * 1024 * 1024
        ),
        name="hessian_exchange",
    )(*operands)
    return jnp.transpose(result, (1, 0, 2))


def solution(mesh):
    in_specs = (
        P(("morton", "sub"), None, None),
        P(("morton", "sub"), None),
        P(("morton", "sub")),
        P(("morton", "sub")),
        P(("morton", "sub")),
        P(("morton", "sub")),
        P(("morton", "sub"), None),
        P(("morton", "sub"), None),
        P(("morton", "sub"), None),
    )
    out_specs = P(("morton", "sub"), None, None)
    return jax.shard_map(
        per_device, mesh=mesh, in_specs=in_specs, out_specs=out_specs, check_vma=False
    )
```

time: 41.8 us -> 40.5 us (0.969)
  the two profiles are of different devices: /device:TPU:49 before, /device:TPU:41 now
where the time goes in v3:
time: 40.5 us; the launch traced here: 40.4 us
  Pallas kernels  39.6 us (98%)
  local copies, waits for them, and re-layouts  0.75 us (2%)
    pallas_call x1, Pallas kernels, per_device(): pl.pallas_call(functools.partial(kernel, ranges), out_shape=jax.ShapeDtyp...  39.6 us

profile of v3, /device:TPU:41, one launch (start us, length us, event | category | flops | bytes accessed | tf_op | source)
XLA Modules:
  0.0 40.4 jit_solution(2638876910768221590)
XLA Ops:
  0.0 39.6 %hessian_exchange.1 = f32[3,64,512]{2,1,0:T(8,128)S(1)} custom-call(f32[3,64,512]{2,1,0:T(8,128)} %bitcast.10, f32[64,512]{1,0:T(8,128)} %jac_hbm.1, f32[1,64]{1,0:T(1,128)} %bitcast.14, f32[1,64]{1,0:T(1,128)} %bitcast.15, s32[1,64]{1,0:T(1,128)} %bitcast.16, s32[1,64]{1,0:T(1,128)} %bitcast.17, s32[6,64]{1,0:T(8,128)} %bitcast.11, s32[6,64]{1,0:T(8,128)} %bitcast.12, ...), custom_call_target="tpu_custom_call" | custom-call | tf_op jit(solution)/shard_map/hessian_exchange/pallas_call | solution.py:443
  39.6 0.7 %copy.16 = f32[64,3,512]{2,0,1:T(8,128)} copy(f32[64,3,512]{2,0,1:T(8,128)S(1)} %bitcast.9) | data formatting | bytes 786432

commit v4 on v3

--- a/solution.py
+++ b/solution.py
@@ -15,10 +15,11 @@
 F32 = jnp.float32
 BF16 = jnp.bfloat16
 MESH = pl.DeviceIdType.MESH
-STEPS = (1, 3, 2, 0)
-SELF = 10
-OTHERS = (6, 8, 7, 0, 2, 3, 5, 1, 4, 9, 11)
-ARRIVALS = (3, 2, 0, 1)
+STEPS = (2, 1, 3, 0)
+SELF = 7
+OTHERS = tuple(q for q in range(PEERS) if q != SELF)
+F_BATCHES = ((5, 6), (4, 7), (8, 9, 10, 11), (0, 1, 2, 3))
+A_BATCHES = ((0, 1), (2, 3), (8, 9, 10, 11), (4, 5, 6, 7))
 PAIRS = {(0, 0): 0, (1, 1): 1, (2, 2): 2, (0, 1): 3, (0, 2): 4, (1, 2): 5}
 
 
@@ -27,7 +28,7 @@
 
 
 def mirror(q):
-    return 3 * STEPS.index((4 - STEPS[q // 3]) % 4) + 2 - q % 3
+    return q - q % 4 + STEPS.index((4 - STEPS[q % 4]) % 4)
 
 
 def tables():
@@ -54,8 +55,8 @@
             fill[lanes, cols] = spread.T
             unfill[lanes, cols] = spread
     twice = np.concatenate([pick, pick], axis=2).reshape(512, 768)
-    inject = pick.reshape(512, 3, 128).transpose(1, 2, 0)
-    inject = np.concatenate([inject, inject], axis=1).reshape(768, 512)
+    inject = pick.reshape(512, 3, 128).transpose(1, 2, 0)[1:]
+    inject = np.concatenate([inject, inject], axis=1).reshape(512, 512)
     before = np.triu(np.ones((ROWS, ROWS), np.float32), 1)
     stacked = (np.concatenate([t, t], axis=0) for t in (fill, unfill))
     return [jnp.asarray(t, BF16) for t in (twice, inject, *stacked, before)]
@@ -91,24 +92,24 @@
     x, jac, mu, lam, level, live, nb, kind, quad,
     twice, inject, fill, unfill, before,
     tile_s, code_b, coef, table, sel_t, place, place_t, lists, lists_in,
-    fsend, frecv, asend, arecv, gathered, leaving, sym, inj, back,
+    fsend, frecv, asend, arecv, gathered, leaving, sym, terms, edge, inj, back,
     in_sem, list_ssem, list_rsem, f_ssem, f_rsem, a_ssem, a_rsem,
 ):
     me_m = lax.axis_index("morton")
     me_x = lax.axis_index("sub")
-    has_low = me_m > 0
-    has_high = me_m < ranges - 1
-    present = 3 + 4 * has_low.astype(jnp.int32) + 4 * has_high.astype(jnp.int32)
+    across = lax.rem(me_m, 2) * 2 - 1
+    has_across = jnp.logical_and(me_m > 0, me_m < ranges - 1)
+    present = 7 + 4 * has_across.astype(jnp.int32)
     low_half = lane_iota((1, 128)) < 64
 
     def device(q):
-        return (me_m + (q % 3 - 1), lax.rem(me_x + STEPS[q // 3], 4))
+        return (me_m + across * (1 - q // 4), lax.rem(me_x + STEPS[q % 4], 4))
 
     def guarded(q, act):
-        if q % 3 == 1:
+        if q // 4 == 0:
+            pl.when(has_across)(act)
+        else:
             act()
-        else:
-            pl.when(has_low if q % 3 == 0 else has_high)(act)
 
     sends = []
 
@@ -143,8 +144,8 @@
         for load in loads[first:last]:
             load.wait()
 
-    def clear(first):
-        for q in range(first, PEERS, 3):
+    def clear():
+        for q in range(4):
             frecv[q] = jnp.zeros((96, 128), F32)
             arecv[q] = jnp.zeros((96, 128), F32)
             lists_in[q] = jnp.zeros((8, 128), F32)
@@ -155,8 +156,8 @@
         want = nb[...]
         owner = want >> 6
         step = (owner - me_x) & 3
-        group = jnp.where(step == 1, 0, jnp.where(step == 3, 1, jnp.where(step == 2, 2, 3)))
-        peer = group * 3 + ((owner >> 2) - me_m + 1)
+        place_of = jnp.where(step == 2, 0, jnp.where(step == 0, 3, jnp.where(step == 1, 1, 2)))
+        peer = (1 - across * ((owner >> 2) - me_m)) * 4 + place_of
         opposite = row_iota((6, 64)) ^ 1
         tile_s[0:6, 0:64] = (peer * 512 + opposite * 64 + (want & 63)).astype(F32)
         packed = tile_s[...]
@@ -184,10 +185,9 @@
 
     def prepare(slot):
         slot_col = jnp.broadcast_to(slot, (8, ROWS)).T[:, 0:1]
-        lanes = lane_iota((ROWS, ROWS))
-        lanes = jnp.where(lanes < 192, lanes, lanes - 192).astype(F32)
-        for i in range(4):
-            place_t[i] = one_hot(lanes == slot_col - 192.0 * i)
+        lanes = (lane_iota((ROWS, 512)) & 255).astype(F32)
+        for i in range(3):
+            place_t[i] = one_hot(lanes == slot_col - 256.0 * i)
         loaded(2, 8)
         scale = jnp.left_shift(jnp.ones((1, 64), jnp.int32), level[...]).astype(F32) * 0.25
         tile_s[...] = jnp.zeros((8, 128), F32)
@@ -227,25 +227,24 @@
         third = jnp.concatenate([jnp.where(low_half, tail, other), jnp.where(low_half, other, tail)], axis=0)
         return jnp.concatenate([message[0:64], third], axis=1)
 
-    def gather(i):
+    def gather(batch):
         lane_row = lane_iota((64, ROWS)).astype(F32)
         chosen = []
-        for q in range(3 * i, 3 * i + 3):
+        for q in batch:
             column = lists_in[q].T[0:64, 0:1]
             chosen.append(one_hot(lane_row == column))
         chosen = jnp.concatenate(chosen, axis=0)
         rows = dot(jnp.concatenate([chosen, chosen], axis=1), table[...])
-        for n in range(3):
-            q = 3 * i + n
+        for n, q in enumerate(batch):
             pack(frecv if q == SELF else fsend, q, rows[64 * n:64 * n + 64])
 
     def selection(i):
-        a, b, c = (lists_in[q][0:1] for q in range(3 * i, 3 * i + 3))
-        ids = [jnp.where(low_half, u, v) for u, v in ((a, b), (c, a), (b, c))]
-        sel_t[i] = one_hot(row_iota((ROWS, ROWS)).astype(F32) == jnp.concatenate(ids, axis=1))
+        a, b, c, d = (lists_in[q][0:1] for q in range(4 * i, 4 * i + 4))
+        ids = [jnp.where(low_half, a, b), jnp.where(low_half, c, d)] * 2
+        sel_t[i] = one_hot(row_iota((ROWS, 512)).astype(F32) == jnp.concatenate(ids, axis=1))
 
     def collect(i, weights, messages, first):
-        rows = jnp.concatenate([unpack(messages[q]) for q in range(3 * i, 3 * i + 3)], axis=0)
+        rows = jnp.concatenate([unpack(messages[q]) for q in range(4 * i, 4 * i + 4)], axis=0)
         part = dot(weights[i], split(rows, 0))
         gathered[...] = part if first else gathered[...] + part
 
@@ -308,30 +307,55 @@
 
     def ghosts():
         parts = by_quadrant(gathered[...], fill)
-        for a in range(3):
+        edge[...] = sided(parts, 0, -1.0).reshape(3, 64, 128)
+        for a in (1, 2):
             sides = split(sided(parts, a, -1.0), 1)
-            inj[a] = dot(sides, inject[256 * a:256 * a + 256]).reshape(3, 64, 512)
+            inj[a - 1] = dot(sides, inject[256 * a - 256:256 * a]).reshape(3, 64, 512)
+
+    def at_ends(v, t):
+        return jnp.where(low_half, v, 0.0) if t == 0 else jnp.where(low_half, 0.0, v)
 
     def stress(i, _):
-        rows = pl.ds(pl.multiple_of(i * 8, 8), 8)
+        rows = pl.ds(pl.multiple_of(i * 16, 16), 16)
         for t in range(4):
             cols = slice(128 * t, 128 * t + 128)
             shear = jac[rows, cols]
-            diag = [sym[a, rows, cols] + inj[a, a, rows, cols] for a in range(3)]
-            trace = coef[0, rows] * (diag[0] + diag[1] + diag[2])
-            for a in range(3):
-                sym[a, rows, cols] = trace + 2.0 * shear * diag[a]
-                for b in range(a + 1, 3):
-                    both = sym[pair(a, b), rows, cols] + inj[a, b, rows, cols] + inj[b, a, rows, cols]
-                    sym[pair(a, b), rows, cols] = shear * both
+            e = [sym[k, rows, cols] for k in range(6)]
+            if t in (0, 3):
+                for c in range(3):
+                    e[pair(c, 0)] = e[pair(c, 0)] + at_ends(edge[c, rows], t)
+            for a in (1, 2):
+                for c in range(3):
+                    e[pair(c, a)] = e[pair(c, a)] + inj[a - 1, c, rows, cols]
+            trace = coef[0, rows] * (e[0] + e[1] + e[2])
+            for k in range(6):
+                value = trace + 2.0 * shear * e[k] if k < 3 else shear * e[k]
+                sym[k, rows, cols] = value
+                if k > 0:
+                    high = value.astype(BF16)
+                    terms[0, k - 1, rows, cols] = high
+                    terms[1, k - 1, rows, cols] = (value - high.astype(F32)).astype(BF16)
         return 0
 
     def adjoint_faces():
-        bars = []
-        for a in range(3):
-            stacked = jnp.concatenate([sym[pair(c, a)] for c in range(3)], axis=0)
-            weights = twice[:, 256 * a:256 * a + 256]
-            layers = dot(split(stacked, 1), jnp.concatenate([weights, weights], axis=0))
+        first = [sym[pair(c, 0), :, 0:128] for c in range(3)]
+        last = [sym[pair(c, 0), :, 384:512] for c in range(3)]
+
+        def swing(v):
+            return pltpu.roll(v, 64, axis=1)
+
+        bars = [
+            jnp.concatenate(
+                [-jnp.where(low_half, first[0], swing(first[1])), -jnp.where(low_half, first[2], swing(first[2]))], axis=1
+            ),
+            jnp.concatenate(
+                [jnp.where(low_half, swing(last[0]), last[1]), jnp.where(low_half, swing(last[2]), last[2])], axis=1
+            ),
+        ]
+        for a in (1, 2):
+            stacked = [terms[part, pair(c, a) - 1] for part in range(2) for c in range(3)]
+            layers = dot(jnp.concatenate(stacked, axis=0), twice[:, 256 * a:256 * a + 256])
+            layers = layers[0:192] + layers[192:384]
             for side in range(2):
                 cut = layers[:, 128 * side:128 * side + 128]
                 if side == 0:
@@ -340,11 +364,10 @@
         parts = by_quadrant(jnp.concatenate(bars, axis=0), unfill)
         leaving[...] = split(jnp.concatenate(parts, axis=1), 0)
 
-    def scatter(i):
-        chosen = place[192 * i:192 * i + 192]
+    def scatter(batch):
+        chosen = place[64 * batch[0]:64 * batch[-1] + 64]
         rows = dot(jnp.concatenate([chosen, chosen], axis=1), leaving[...])
-        for n in range(3):
-            q = 3 * i + n
+        for n, q in enumerate(batch):
             pack(arecv if q == SELF else asend, q, rows[64 * n:64 * n + 64])
 
     def outer(i, _):
@@ -361,19 +384,23 @@
     def land():
         rows = gathered[...]
         parts = [rows[:, 0:128], rows[:, 128:256]]
-        sides = jnp.concatenate([split(sided(parts, a, 1.0), 1) for a in range(3)], axis=1)
-        total = dot(sides, inject[...])
-        alive = jnp.concatenate([coef[2]] * 4, axis=1)
+        ends = sided(parts, 0, 1.0)
+        sides = split(jnp.concatenate([sided(parts, a, 1.0) for a in (1, 2)], axis=1), 0)
+        total = dot(sides, jnp.concatenate([inject[0:128], inject[256:384]], axis=0))
         for c in range(3):
-            out_ref[c] = (back[c] + total[64 * c:64 * c + 64]) * alive
+            for t in range(4):
+                cols = slice(128 * t, 128 * t + 128)
+                value = back[c, :, cols] + (total[64 * c:64 * c + 64, cols] + total[192 + 64 * c:256 + 64 * c, cols])
+                if t in (0, 3):
+                    value = value + at_ends(ends[64 * c:64 * c + 64], t)
+                out_ref[c, :, cols] = value * coef[2]
 
     for load in loads:
         load.start()
     barrier = pltpu.get_barrier_semaphore()
     for q in OTHERS:
         guarded(q, lambda q=q: pl.semaphore_signal(barrier, inc=1, device_id=device(q), device_id_type=MESH))
-    pl.when(jnp.logical_not(has_low))(lambda: clear(0))
-    pl.when(jnp.logical_not(has_high))(lambda: clear(2))
+    pl.when(jnp.logical_not(has_across))(clear)
     slot = request()
     pl.semaphore_wait(barrier, present)
     for q in OTHERS:
@@ -381,37 +408,37 @@
     lists_in[SELF] = lists[SELF]
     prepare(slot)
 
-    for i in (2, 0, 1, 3):
-        for q in range(3 * i, 3 * i + 3):
+    for batch in F_BATCHES:
+        for q in batch:
             if q != SELF:
                 arrive(q, lists_in, list_ssem, list_rsem)
-        gather(i)
-        for q in range(3 * i, 3 * i + 3):
+        gather(batch)
+        for q in batch:
             if q != SELF:
                 send(q, fsend, frecv, f_ssem, f_rsem)
 
     loaded(10, 11)
     lax.fori_loop(0, 8, inner, 0)
-    for i in range(4):
+    for i in range(3):
         selection(i)
     loaded(11, 14)
-    for n, i in enumerate(ARRIVALS):
-        for q in range(3 * i, 3 * i + 3):
+    for n, i in enumerate((1, 0, 2)):
+        for q in range(4 * i, 4 * i + 4):
             if q != SELF:
                 arrive(q, frecv, f_ssem, f_rsem)
         collect(i, place_t, frecv, n == 0)
     ghosts()
-    lax.fori_loop(0, 8, stress, 0)
+    lax.fori_loop(0, 4, stress, 0)
     adjoint_faces()
-    for i in (2, 0, 1, 3):
-        scatter(i)
-        for q in range(3 * i, 3 * i + 3):
+    for batch in A_BATCHES:
+        scatter(batch)
+        for q in batch:
             if q != SELF:
                 send(q, asend, arecv, a_ssem, a_rsem)
 
     lax.fori_loop(0, 8, outer, 0)
-    for n, i in enumerate(ARRIVALS):
-        for q in range(3 * i, 3 * i + 3):
+    for n, i in enumerate((0, 1, 2)):
+        for q in range(4 * i, 4 * i + 4):
             if q != SELF:
                 arrive(q, arecv, a_ssem, a_rsem)
         collect(i, sel_t, arecv, n == 0)
@@ -451,9 +478,9 @@
             pltpu.VMEM((ROWS, 128), F32),
             pltpu.VMEM((3, 64, 128), F32),
             pltpu.VMEM((2 * ROWS, 256), BF16),
-            pltpu.VMEM((4, ROWS, ROWS), BF16),
+            pltpu.VMEM((3, ROWS, 512), BF16),
             pltpu.VMEM((SLOTS, ROWS), BF16),
-            pltpu.VMEM((4, ROWS, ROWS), BF16),
+            pltpu.VMEM((3, ROWS, 512), BF16),
             short,
             short,
             message,
@@ -463,7 +490,9 @@
             pltpu.VMEM((ROWS, 256), F32),
             pltpu.VMEM((2 * ROWS, 256), BF16),
             pltpu.VMEM((6, 64, 512), F32),
-            pltpu.VMEM((3, 3, 64, 512), F32),
+            pltpu.VMEM((2, 5, 64, 512), BF16),
+            pltpu.VMEM((3, 64, 128), F32),
+            pltpu.VMEM((2, 3, 64, 512), F32),
             pltpu.VMEM((3, 64, 512), F32),
             pltpu.SemaphoreType.DMA((len(operands),)),
             peers,

time: 40.5 us -> 39.9 us (0.985)
  the two profiles are of different devices: /device:TPU:41 before, /device:TPU:40 now
where the time goes in v4:
time: 39.9 us; the launch traced here: 39.8 us
  Pallas kernels  39 us (98%)
  local copies, waits for them, and re-layouts  0.75 us (2%)
    pallas_call x1, Pallas kernels, per_device(): pl.pallas_call(functools.partial(kernel, ranges), out_shape=jax.ShapeDtyp...  39 us

profile of v4, /device:TPU:40, one launch (start us, length us, event | category | flops | bytes accessed | tf_op | source)
XLA Modules:
  0.0 39.8 jit_solution(12786541208557595067)
XLA Ops:
  0.0 39.0 %hessian_exchange.1 = f32[3,64,512]{2,1,0:T(8,128)S(1)} custom-call(f32[3,64,512]{2,1,0:T(8,128)} %bitcast.10, f32[64,512]{1,0:T(8,128)} %jac_hbm.1, f32[1,64]{1,0:T(1,128)} %bitcast.14, f32[1,64]{1,0:T(1,128)} %bitcast.15, s32[1,64]{1,0:T(1,128)} %bitcast.16, s32[1,64]{1,0:T(1,128)} %bitcast.17, s32[6,64]{1,0:T(8,128)} %bitcast.11, s32[6,64]{1,0:T(8,128)} %bitcast.12, ...), custom_call_target="tpu_custom_call" | custom-call | tf_op jit(solution)/shard_map/hessian_exchange/pallas_call | solution.py:470
  39.0 0.7 %copy.16 = f32[64,3,512]{2,0,1:T(8,128)} copy(f32[64,3,512]{2,0,1:T(8,128)S(1)} %bitcast.9) | data formatting | bytes 786432

commit v5 on v4

--- a/solution.py
+++ b/solution.py
@@ -113,17 +113,17 @@
 
     sends = []
 
-    def send(q, src, dst, ssem, rsem):
+    def send(q, src, dst, ssem, rsem, rows=96):
         copy = pltpu.make_async_remote_copy(
-            src_ref=src.at[q], dst_ref=dst.at[mirror(q)], send_sem=ssem.at[q], recv_sem=rsem.at[mirror(q)],
+            src_ref=src.at[q, 0:rows], dst_ref=dst.at[mirror(q), 0:rows], send_sem=ssem.at[q], recv_sem=rsem.at[mirror(q)],
             device_id=device(q), device_id_type=MESH,
         )
         guarded(q, copy.start)
         sends.append((q, copy))
 
-    def arrive(q, dst, ssem, rsem):
+    def arrive(q, dst, ssem, rsem, rows=96):
         copy = pltpu.make_async_remote_copy(
-            src_ref=dst.at[q], dst_ref=dst.at[q], send_sem=ssem.at[q], recv_sem=rsem.at[q],
+            src_ref=dst.at[q, 0:rows], dst_ref=dst.at[q, 0:rows], send_sem=ssem.at[q], recv_sem=rsem.at[q],
             device_id=device(q), device_id_type=MESH,
         )
         guarded(q, copy.wait_recv)
@@ -231,7 +231,7 @@
         lane_row = lane_iota((64, ROWS)).astype(F32)
         chosen = []
         for q in batch:
-            column = lists_in[q].T[0:64, 0:1]
+            column = jnp.broadcast_to(lists_in[q, 0:1], (8, 128)).T[0:64, 0:1]
             chosen.append(one_hot(lane_row == column))
         chosen = jnp.concatenate(chosen, axis=0)
         rows = dot(jnp.concatenate([chosen, chosen], axis=1), table[...])
@@ -239,7 +239,7 @@
             pack(frecv if q == SELF else fsend, q, rows[64 * n:64 * n + 64])
 
     def selection(i):
-        a, b, c, d = (lists_in[q][0:1] for q in range(4 * i, 4 * i + 4))
+        a, b, c, d = (lists_in[q, 0:1] for q in range(4 * i, 4 * i + 4))
         ids = [jnp.where(low_half, a, b), jnp.where(low_half, c, d)] * 2
         sel_t[i] = one_hot(row_iota((ROWS, 512)).astype(F32) == jnp.concatenate(ids, axis=1))
 
@@ -395,23 +395,25 @@
                     value = value + at_ends(ends[64 * c:64 * c + 64], t)
                 out_ref[c, :, cols] = value * coef[2]
 
-    for load in loads:
-        load.start()
+    loads[0].start()
+    loads[1].start()
     barrier = pltpu.get_barrier_semaphore()
     for q in OTHERS:
         guarded(q, lambda q=q: pl.semaphore_signal(barrier, inc=1, device_id=device(q), device_id_type=MESH))
+    for load in loads[2:]:
+        load.start()
     pl.when(jnp.logical_not(has_across))(clear)
     slot = request()
     pl.semaphore_wait(barrier, present)
     for q in OTHERS:
-        send(q, lists, lists_in, list_ssem, list_rsem)
+        send(q, lists, lists_in, list_ssem, list_rsem, 1)
     lists_in[SELF] = lists[SELF]
     prepare(slot)
 
     for batch in F_BATCHES:
         for q in batch:
             if q != SELF:
-                arrive(q, lists_in, list_ssem, list_rsem)
+                arrive(q, lists_in, list_ssem, list_rsem, 1)
         gather(batch)
         for q in batch:
             if q != SELF:

time: 39.9 us -> 39.7 us (level)
  no operation moved by 1% of the time
where the time goes in v5:
time: 39.7 us; the launch traced here: 39.5 us
  Pallas kernels  38.8 us (98%)
  local copies, waits for them, and re-layouts  0.75 us (2%)
    pallas_call x1, Pallas kernels, per_device(): pl.pallas_call(functools.partial(kernel, ranges), out_shape=jax.ShapeDtyp...  38.8 us

profile of v5, /device:TPU:40, one launch (start us, length us, event | category | flops | bytes accessed | tf_op | source)
XLA Modules:
  0.0 39.5 jit_solution(16062588026387334755)
XLA Ops:
  0.0 38.8 %hessian_exchange.1 = f32[3,64,512]{2,1,0:T(8,128)S(1)} custom-call(f32[3,64,512]{2,1,0:T(8,128)} %bitcast.10, f32[64,512]{1,0:T(8,128)} %jac_hbm.1, f32[1,64]{1,0:T(1,128)} %bitcast.14, f32[1,64]{1,0:T(1,128)} %bitcast.15, s32[1,64]{1,0:T(1,128)} %bitcast.16, s32[1,64]{1,0:T(1,128)} %bitcast.17, s32[6,64]{1,0:T(8,128)} %bitcast.11, s32[6,64]{1,0:T(8,128)} %bitcast.12, ...), custom_call_target="tpu_custom_call" | custom-call | tf_op jit(solution)/shard_map/hessian_exchange/pallas_call | solution.py:472
  38.8 0.7 %copy.16 = f32[64,3,512]{2,0,1:T(8,128)} copy(f32[64,3,512]{2,0,1:T(8,128)S(1)} %bitcast.9) | data formatting | bytes 786432

commit v6 on v5

--- a/solution.py
+++ b/solution.py
@@ -424,7 +424,7 @@
     for i in range(3):
         selection(i)
     loaded(11, 14)
-    for n, i in enumerate((1, 0, 2)):
+    for n, i in enumerate((1, 2, 0)):
         for q in range(4 * i, 4 * i + 4):
             if q != SELF:
                 arrive(q, frecv, f_ssem, f_rsem)
@@ -439,7 +439,7 @@
                 send(q, asend, arecv, a_ssem, a_rsem)
 
     lax.fori_loop(0, 8, outer, 0)
-    for n, i in enumerate((0, 1, 2)):
+    for n, i in enumerate((0, 2, 1)):
         for q in range(4 * i, 4 * i + 4):
             if q != SELF:
                 arrive(q, arecv, a_ssem, a_rsem)

time: 39.7 us -> 39.4 us (level)
  the two profiles are of different devices: /device:TPU:40 before, /device:TPU:49 now
where the time goes in v6:
time: 39.4 us; the launch traced here: 39.1 us
  Pallas kernels  38.3 us (97%)
  local copies, waits for them, and re-layouts  0.75 us (2%)
    pallas_call x1, Pallas kernels, per_device(): pl.pallas_call(functools.partial(kernel, ranges), out_shape=jax.ShapeDtyp...  38.3 us

profile of v6, /device:TPU:49, one launch (start us, length us, event | category | flops | bytes accessed | tf_op | source)
XLA Modules:
  0.0 39.1 jit_solution(3158596870867814150)
XLA Ops:
  0.0 38.3 %hessian_exchange.1 = f32[3,64,512]{2,1,0:T(8,128)S(1)} custom-call(f32[3,64,512]{2,1,0:T(8,128)} %bitcast.10, f32[64,512]{1,0:T(8,128)} %jac_hbm.1, f32[1,64]{1,0:T(1,128)} %bitcast.14, f32[1,64]{1,0:T(1,128)} %bitcast.15, s32[1,64]{1,0:T(1,128)} %bitcast.16, s32[1,64]{1,0:T(1,128)} %bitcast.17, s32[6,64]{1,0:T(8,128)} %bitcast.11, s32[6,64]{1,0:T(8,128)} %bitcast.12, ...), custom_call_target="tpu_custom_call" | custom-call | tf_op jit(solution)/shard_map/hessian_exchange/pallas_call | solution.py:472
  38.3 0.7 %copy.16 = f32[64,3,512]{2,0,1:T(8,128)} copy(f32[64,3,512]{2,0,1:T(8,128)S(1)} %bitcast.9) | data formatting | bytes 786432

commit v7 on v6

--- a/solution.py
+++ b/solution.py
@@ -185,9 +185,9 @@
 
     def prepare(slot):
         slot_col = jnp.broadcast_to(slot, (8, ROWS)).T[:, 0:1]
-        lanes = (lane_iota((ROWS, 512)) & 255).astype(F32)
-        for i in range(3):
-            place_t[i] = one_hot(lanes == slot_col - 256.0 * i)
+        lanes = (lane_iota((ROWS, 256)) & 127).astype(F32)
+        for i in range(6):
+            place_t[i] = one_hot(lanes == slot_col - 128.0 * i)
         loaded(2, 8)
         scale = jnp.left_shift(jnp.ones((1, 64), jnp.int32), level[...]).astype(F32) * 0.25
         tile_s[...] = jnp.zeros((8, 128), F32)
@@ -201,8 +201,8 @@
         kinds = kind[...]
         tile_s[0:6, 0:64] = jnp.where(kinds == 1, 4, jnp.where(kinds == 2, quad[...], -1)).astype(F32)
         flat = tile_s[...].T
-        for f in range(6):
-            code_b[64 * f:64 * f + 64] = jnp.broadcast_to(flat[0:64, f:f + 1], (64, 128))
+        codes = jnp.concatenate([jnp.broadcast_to(flat[0:64, f:f + 1], (64, 128)) for f in range(6)], axis=0)
+        code_b[...] = codes
         loaded(8, 9)
         alive = jnp.concatenate([coef[2]] * 4, axis=1)
         for c in range(3):
@@ -239,12 +239,23 @@
             pack(frecv if q == SELF else fsend, q, rows[64 * n:64 * n + 64])
 
     def selection(i):
-        a, b, c, d = (lists_in[q, 0:1] for q in range(4 * i, 4 * i + 4))
-        ids = [jnp.where(low_half, a, b), jnp.where(low_half, c, d)] * 2
-        sel_t[i] = one_hot(row_iota((ROWS, 512)).astype(F32) == jnp.concatenate(ids, axis=1))
+        ids = jnp.where(low_half, lists_in[2 * i, 0:1], lists_in[2 * i + 1, 0:1])
+        sel_t[i] = one_hot(row_iota((ROWS, 256)).astype(F32) == jnp.concatenate([ids, ids], axis=1))
+
+    def by_quadrant(rows, weights, code):
+        masks = [code == float(q) for q in range(5)]
+        result = []
+        for half in range(2):
+            value = rows[:, 128 * half:128 * half + 128]
+            spread = dot(split(value, 1), weights[...])
+            value = jnp.where(masks[4], value, 0.0)
+            for q in range(4):
+                value = jnp.where(masks[q], spread[:, 128 * q:128 * q + 128], value)
+            result.append(value)
+        return jnp.concatenate(result, axis=1)
 
     def collect(i, weights, messages, first):
-        rows = jnp.concatenate([unpack(messages[q]) for q in range(4 * i, 4 * i + 4)], axis=0)
+        rows = jnp.concatenate([unpack(messages[2 * i]), unpack(messages[2 * i + 1])], axis=0)
         part = dot(weights[i], split(rows, 0))
         gathered[...] = part if first else gathered[...] + part
 
@@ -279,20 +290,6 @@
             jac[rows, cols] = coef[1, rows] - coef[0, rows] * jnp.log(jac[rows, cols])
         return 0
 
-    def by_quadrant(parts, weights):
-        code = code_b[...]
-        masks = [code == float(q) for q in range(5)]
-        result = []
-        for half in range(2):
-            cut = slice(128 * half, 128 * half + 128)
-            value = parts[:, cut]
-            spread = dot(split(value, 1), weights[...])
-            value = jnp.where(masks[4], value, 0.0)
-            for q in range(4):
-                value = jnp.where(masks[q], spread[:, 128 * q:128 * q + 128], value)
-            result.append(value)
-        return result
-
     def sided(parts, a, sign):
         low = [sign * part[128 * a:128 * a + 64] for part in parts]
         high = [part[128 * a + 64:128 * a + 128] for part in parts]
@@ -306,7 +303,8 @@
         )
 
     def ghosts():
-        parts = by_quadrant(gathered[...], fill)
+        rows = by_quadrant(gathered[...], fill, code_b[...])
+        parts = [rows[:, 0:128], rows[:, 128:256]]
         edge[...] = sided(parts, 0, -1.0).reshape(3, 64, 128)
         for a in (1, 2):
             sides = split(sided(parts, a, -1.0), 1)
@@ -361,11 +359,11 @@
                 if side == 0:
                     cut = -cut
                 bars.append(jnp.concatenate([jnp.where(low_half, cut[0:64], cut[64:128]), cut[128:192]], axis=1))
-        parts = by_quadrant(jnp.concatenate(bars, axis=0), unfill)
-        leaving[...] = split(jnp.concatenate(parts, axis=1), 0)
+        leaving[...] = split(by_quadrant(jnp.concatenate(bars, axis=0), unfill, code_b[...]), 0)
 
     def scatter(batch):
-        chosen = place[64 * batch[0]:64 * batch[-1] + 64]
+        slots = slice(64 * batch[0], 64 * batch[-1] + 64)
+        chosen = place[slots]
         rows = dot(jnp.concatenate([chosen, chosen], axis=1), leaving[...])
         for n, q in enumerate(batch):
             pack(arecv if q == SELF else asend, q, rows[64 * n:64 * n + 64])
@@ -421,11 +419,11 @@
 
     loaded(10, 11)
     lax.fori_loop(0, 8, inner, 0)
-    for i in range(3):
+    for i in range(6):
         selection(i)
     loaded(11, 14)
-    for n, i in enumerate((1, 2, 0)):
-        for q in range(4 * i, 4 * i + 4):
+    for n, i in enumerate((2, 3, 4, 5, 0, 1)):
+        for q in (2 * i, 2 * i + 1):
             if q != SELF:
                 arrive(q, frecv, f_ssem, f_rsem)
         collect(i, place_t, frecv, n == 0)
@@ -439,8 +437,8 @@
                 send(q, asend, arecv, a_ssem, a_rsem)
 
     lax.fori_loop(0, 8, outer, 0)
-    for n, i in enumerate((0, 2, 1)):
-        for q in range(4 * i, 4 * i + 4):
+    for n, i in enumerate((0, 1, 4, 5, 2, 3)):
+        for q in (2 * i, 2 * i + 1):
             if q != SELF:
                 arrive(q, arecv, a_ssem, a_rsem)
         collect(i, sel_t, arecv, n == 0)
@@ -480,9 +478,9 @@
             pltpu.VMEM((ROWS, 128), F32),
             pltpu.VMEM((3, 64, 128), F32),
             pltpu.VMEM((2 * ROWS, 256), BF16),
-            pltpu.VMEM((3, ROWS, 512), BF16),
+            pltpu.VMEM((6, ROWS, 256), BF16),
             pltpu.VMEM((SLOTS, ROWS), BF16),
-            pltpu.VMEM((3, ROWS, 512), BF16),
+            pltpu.VMEM((6, ROWS, 256), BF16),
             short,
             short,
             message,

time: 39.4 us -> 39.7 us (level)
  Pallas kernels: 38.3 us -> 38.8 us
    pallas_call x1, Pallas kernels: 38.3 us -> 38.8 us  [per_device(): pl.pallas_call(functools.partial(kernel, ranges), out_shape=jax.ShapeDtyp...]
where the time goes in v7:
time: 39.7 us; the launch traced here: 39.5 us
  Pallas kernels  38.8 us (98%)
  local copies, waits for them, and re-layouts  0.75 us (2%)
    pallas_call x1, Pallas kernels, per_device(): pl.pallas_call(functools.partial(kernel, ranges), out_shape=jax.ShapeDtyp...  38.8 us

profile of v7, /device:TPU:49, one launch (start us, length us, event | category | flops | bytes accessed | tf_op | source)
XLA Modules:
  0.0 39.5 jit_solution(4879818265132482410)
XLA Ops:
  0.0 38.8 %hessian_exchange.1 = f32[3,64,512]{2,1,0:T(8,128)S(1)} custom-call(f32[3,64,512]{2,1,0:T(8,128)} %bitcast.10, f32[64,512]{1,0:T(8,128)} %jac_hbm.1, f32[1,64]{1,0:T(1,128)} %bitcast.14, f32[1,64]{1,0:T(1,128)} %bitcast.15, s32[1,64]{1,0:T(1,128)} %bitcast.16, s32[1,64]{1,0:T(1,128)} %bitcast.17, s32[6,64]{1,0:T(8,128)} %bitcast.11, s32[6,64]{1,0:T(8,128)} %bitcast.12, ...), custom_call_target="tpu_custom_call" | custom-call | tf_op jit(solution)/shard_map/hessian_exchange/pallas_call | solution.py:470
  38.8 0.7 %copy.16 = f32[64,3,512]{2,0,1:T(8,128)} copy(f32[64,3,512]{2,0,1:T(8,128)S(1)} %bitcast.9) | data formatting | bytes 786432
